TPU v7x, 32 devices: a whole 2x2x4 slice. The times are simulated.
32 devices in a mesh: ctl: 4 (over z), seq: 8 (over y, x, core).
Axes of the slice: x: 2, y: 2, z: 4, core: 2. Of those that a mesh axis runs over, the one named last changes fastest.
Arguments:
- control_hidden_state: bfloat16 [8, 64, 48, 3072], P('seq', None, 'ctl'), may hold values from -60 to 60
- patch_segment_labels: int32 [8, 64, 48], P('seq', None, 'ctl'), may hold values from 0 to 149
- patch_depth_levels: int32 [8, 64, 48], P('seq', None, 'ctl'), may hold values from 0 to 255
- timestep: int32 [8], replicated, may hold values from 0 to 999
- segment_label_embedding: bfloat16 [150, 3072], replicated, may hold values from -3 to 3
- depth_level_embedding: bfloat16 [256, 3072], replicated, may hold values from -3 to 3
- timestep_weight: bfloat16 [256, 3072], replicated, may hold values from -0.875 to 0.875
- control_norm_gain: float32 [3072], replicated, may hold values from 0.1 to 1.9
- control_output_weight: bfloat16 [3072, 3072], P('ctl'), may hold values from -0.109375 to 0.109375
- transformer_hidden_state: bfloat16 [8, 64, 48, 3072], P('ctl', 'seq'), may hold values from -3 to 3
- query: bfloat16 [8, 64, 48, 2048], P('ctl', 'seq'), may hold values from -5 to 5
- key: bfloat16 [8, 64, 48, 2048], P('ctl', 'seq'), may hold values from -5 to 5
- value: bfloat16 [8, 64, 48, 2048], P('ctl', 'seq'), may hold values from -12 to 12
- attention_output_weight: bfloat16 [2048, 3072], P('ctl'), may hold values from -0.125 to 0.125
Outputs:
- next_hidden: bfloat16 [8, 64, 48, 3072], P('ctl', 'seq')
All inputs are finite; a program needn't handle non-finite values.
Results may differ from a plain program's by a relative error of at most 0.0059.
Values may be sent and summed in bfloat16 or wider, within the bound.
A program may use at most 192 MiB of HBM per device.

v0:
```python
import math

import jax
import jax.numpy as jnp
from jax import lax
from jax.sharding import PartitionSpec as P

HEADS = 16
HEAD_DIM = 128


def time_embed(timestep, timestep_weight):
    half = timestep_weight.shape[0] // 2
    freqs = jnp.exp(-math.log(10000.0) * jnp.arange(half, dtype=jnp.float32) / half)
    angles = timestep.astype(jnp.float32)[:, None] * freqs[None, :]
    features = jnp.concatenate([jnp.cos(angles), jnp.sin(angles)], axis=1).astype(jnp.bfloat16)
    return jax.nn.silu(jnp.dot(features, timestep_weight, preferred_element_type=jnp.float32))


def lookup(indices, table):
    depth_indices = lax.broadcasted_iota(jnp.int32, (1, table.shape[0]), 1)
    onehot = (indices.reshape(-1, 1) == depth_indices).astype(jnp.bfloat16)
    return jnp.dot(onehot, table, preferred_element_type=jnp.float32)


def condition(
    control_hidden_state,
    patch_segment_labels,
    patch_depth_levels,
    segment_label_embedding,
    depth_level_embedding,
    control_norm_gain,
    ctl_gain,
):
    feature_width = control_hidden_state.shape[-1]
    images = control_hidden_state.shape[0]
    mixed = (
        control_hidden_state.reshape(-1, feature_width).astype(jnp.float32)
        + lookup(patch_segment_labels, segment_label_embedding)
        + lookup(patch_depth_levels, depth_level_embedding)
    )
    mixed = mixed.reshape(images, -1, feature_width)
    scale = lax.rsqrt(jnp.mean(mixed * mixed, axis=-1, keepdims=True) + 1e-06)
    normed = mixed * scale * control_norm_gain * (1.0 + ctl_gain[:, None, :])
    return normed.astype(jnp.bfloat16).reshape(control_hidden_state.shape)


def project(normed, control_output_weight):
    feature_width = normed.shape[-1]
    flattened = normed.reshape(-1, feature_width)
    summed = jnp.dot(
        flattened,
        lax.all_gather(control_output_weight, "ctl", axis=0, tiled=True),
        preferred_element_type=jnp.float32,
    )
    return summed.astype(jnp.bfloat16).reshape(
        normed.shape[:-1] + (control_output_weight.shape[1],)
    )


def relayout(field):
    return lax.all_to_all(
        lax.all_to_all(field, "seq", split_axis=1, concat_axis=0, tiled=True),
        "ctl",
        split_axis=0,
        concat_axis=2,
        tiled=True,
    )


def attend(parts):
    query_rows, input_keys, value_rows = parts
    count, grid_rows, grid_cols, local_heads, head_width = query_rows.shape
    length = grid_rows * grid_cols
    shaped = (count, length, local_heads, head_width)
    query_rows = query_rows.reshape(shaped)
    keys_all = input_keys.reshape(shaped)
    values_all = value_rows.reshape(shaped)
    block = math.gcd(length, 512)
    scale = head_width ** (-0.5)

    def one_block(index, output):
        start = index * block
        query_block = lax.dynamic_slice_in_dim(query_rows, start, block, 1)
        scores = (
            jnp.einsum("nqhd,nkhd->nhqk", query_block, keys_all, preferred_element_type=jnp.float32)
            * scale
        )
        peak = jnp.max(scores, axis=3, keepdims=True)
        weights = jnp.exp(scores - peak)
        totals = jnp.sum(weights, axis=3)
        mixed = jnp.einsum(
            "nhqk,nkhd->nqhd",
            weights.astype(jnp.bfloat16),
            values_all,
            preferred_element_type=jnp.float32,
        )
        mixed = mixed / jnp.transpose(totals, (0, 2, 1))[..., None]
        return lax.dynamic_update_slice_in_dim(output, mixed.astype(jnp.bfloat16), start, 1)

    output = lax.fori_loop(0, length // block, one_block, jnp.zeros(shaped, jnp.bfloat16))
    output = output.reshape(count, grid_rows, grid_cols, local_heads, head_width)
    return lax.all_to_all(output, "seq", split_axis=1, concat_axis=3, tiled=True)


def per_device(
    control_hidden_state,
    patch_segment_labels,
    patch_depth_levels,
    timestep,
    segment_label_embedding,
    depth_level_embedding,
    timestep_weight,
    control_norm_gain,
    control_output_weight,
    transformer_hidden_state,
    query,
    key,
    value,
    attention_output_weight,
):
    timestep_gain = time_embed(timestep, timestep_weight)
    images = control_hidden_state.shape[0]
    ctl_gain = lax.dynamic_slice_in_dim(timestep_gain, lax.axis_index("seq") * images, images, 0)
    normed = condition(
        control_hidden_state,
        patch_segment_labels,
        patch_depth_levels,
        segment_label_embedding,
        depth_level_embedding,
        control_norm_gain,
        ctl_gain,
    )
    control_residual = project(relayout(normed), control_output_weight)
    image_group = transformer_hidden_state.shape[0]
    feature_width = transformer_hidden_state.shape[-1]
    transformer_gain = lax.dynamic_slice_in_dim(
        timestep_gain, lax.axis_index("ctl") * image_group, image_group, 0
    )
    split_shape = query.shape[:-1] + (HEADS, HEAD_DIM)
    attended = attend(
        (
            lax.all_to_all(
                query.reshape(split_shape), "seq", split_axis=3, concat_axis=1, tiled=True
            ),
            lax.all_to_all(
                key.reshape(split_shape), "seq", split_axis=3, concat_axis=1, tiled=True
            ),
            lax.all_to_all(
                value.reshape(split_shape), "seq", split_axis=3, concat_axis=1, tiled=True
            ),
        )
    )
    joined = attended.reshape(-1, HEADS * HEAD_DIM)
    projected_rows = jnp.dot(
        joined,
        lax.all_gather(attention_output_weight, "ctl", axis=0, tiled=True),
        preferred_element_type=jnp.float32,
    )
    state_update = (
        projected_rows.reshape(image_group, -1, feature_width) * transformer_gain[:, None, :]
    )
    final_output = (
        transformer_hidden_state.reshape(image_group, -1, feature_width).astype(jnp.float32)
        + state_update
        + control_residual.reshape(image_group, -1, feature_width).astype(jnp.float32)
    )
    return final_output.astype(jnp.bfloat16).reshape(transformer_hidden_state.shape)


def solution(mesh):
    return jax.shard_map(
        per_device,
        mesh=mesh,
        in_specs=(
            P("seq", None, "ctl", None),
            P("seq", None, "ctl"),
            P("seq", None, "ctl"),
            P(),
            P(),
            P(),
            P(),
            P(),
            P("ctl", None),
            P("ctl", "seq", None, None),
            P("ctl", "seq", None, None),
            P("ctl", "seq", None, None),
            P("ctl", "seq", None, None),
            P("ctl", None),
        ),
        out_specs=P("ctl", "seq", None, None),
        check_vma=False,
    )
```

profile of v0, /device:TPU:0, one launch (start us, length us, event | category | flops | bytes accessed | tf_op | source)
XLA Modules:
  0.0 690.3 jit_solution(7412897895298451848)
XLA Ops:
  20.6 33.4 %all-to-all-done.1 = bf16[2,8,48,16,128]{4,2,1,0,3:T(8,128)(2,1)S(1)} async-done(((bf16[2,8,48,16,128]{4,2,1,0,3:T(8,128)(2,1)}), bf16[2,8,48,16,128]{4,2,1,0,3:T(8,128)(2,1)S(1)}, u32[]{:S(2)}, u32[]{:S(2)}) %all-to-all-start.1) | async-done | bytes 3145760 | tf_op jit(solution)/shard_map/all_to_all | solution.py:146
  59.3 9.8 %copy.81 = f32[1,64,12,3072]{3,2,1,0:T(8,128)} copy(bf16[1,64,12,3072]{3,1,2,0:T(8,128)(2,1)} %param.16) | data formatting | bytes 14155776 | tf_op jit(solution)/shard_map/convert_element_type | solution.py:38
  69.0 10.9 %reshape.108 = f32[768,3072]{1,0:T(8,128)} reshape(f32[1,64,12,3072]{3,2,1,0:T(8,128)} %copy.81) | data formatting | bytes 18874368 | tf_op jit(solution)/shard_map/convert_element_type | solution.py:38
  88.2 8.2 %all-to-all-done.2 = bf16[2,8,48,16,128]{4,2,1,0,3:T(8,128)(2,1)} async-done(((bf16[2,8,48,16,128]{4,2,1,0,3:T(8,128)(2,1)}), bf16[2,8,48,16,128]{4,2,1,0,3:T(8,128)(2,1)}, u32[]{:S(2)}, u32[]{:S(2)}) %all-to-all-start.2) | async-done | bytes 3145760 | tf_op jit(solution)/shard_map/all_to_all | solution.py:149
  100.9 7.7 %multiply_reduce_fusion.1 = (f32[768]{0:T(1024)S(1)}, f32[768,3072]{1,0:T(8,128)S(1)}) fusion(bf16[256,3072]{1,0:T(8,128)(2,1)S(1)} %copy-done.5, s32[768]{0:T(1024)S(1)} %eq.34, f32[768,3072]{1,0:T(8,128)} %reshape.108, f32[768,3072]{1,0:T(8,128)} %fusion.27), kind=kOutput, calls=%fused_computation.21 | convolution fusion | flops 1217592576 | bytes 29890560 | tf_op jit(solution)/shard_map/dot_general | solution.py:23
  127.8 11.0 %all-to-all-done = bf16[2,8,48,16,128]{4,2,1,0,3:T(8,128)(2,1)} async-done(((bf16[2,8,48,16,128]{4,2,1,0,3:T(8,128)(2,1)}), bf16[2,8,48,16,128]{4,2,1,0,3:T(8,128)(2,1)}, u32[]{:S(2)}, u32[]{:S(2)}) %all-to-all-start) | async-done | bytes 3145760 | tf_op jit(solution)/shard_map/all_to_all | solution.py:143
  150.2 204.8 %while.13 = (s32[]{:T(128)}, bf16[2,3072,2,128]{3,1,2,0:T(8,128)(2,1)}, bf16[2,3072,2,128]{3,1,2,0:T(8,128)(2,1)}, bf16[2,3072,2,128]{3,1,2,0:T(8,128)(2,1)S(1)}...) while((s32[]{:T(128)}, bf16[2,3072,2,128]{3,1,2,0:T(8,128)(2,1)}, ...), condition=%wide.region_3.0_spmd, body=%wide.region_0.3_spmd.sunk | while | flops 3272077312 | bytes 95461552 | solution.py:101
  150.2 11.3 %multiply_reduce_fusion.3 = (f32[2,2,512]{2,1,0:T(2,128)S(1)}, f32[2,2,512,3072]{3,2,1,0:T(8,128)}) fusion(bf16[2,3072,2,128]{3,1,2,0:T(8,128)(2,1)S(1)} %get-tuple-element.172, bf16[2,3072,2,128]{3,1,2,0:T(8,128)(2,1)} %get-tuple-element.171, s32[]{:T(128)S(6)} %select_n.17), kind=kOutput, calls=%fused_computation.1.clone.1 | convolution fusion | flops 1623193600 | bytes 28844036 | tf_op jit(solution)/shard_map/while/body/eval_jaxpr/nqhd,nkhd->nhqk/dot_general | solution.py:86
  161.5 11.3 %fusion.58 = f32[2,2,512]{2,1,0:T(2,128)S(1)} fusion(f32[2,2,512,3072]{3,2,1,0:T(8,128)} %get-tuple-element.149, f32[2,2,512]{2,1,0:T(2,128)S(1)} %get-tuple-element.150), kind=kLoop, calls=%fused_computation.2.clone.1 | loop fusion | flops 18872320 | bytes 25182208 | tf_op jit(solution)/shard_map/while/body/eval_jaxpr/reduce_sum | solution.py:91
  172.8 11.2 %fusion.59 = bf16[2,3072,2,128]{3,1,2,0:T(8,128)(2,1)} fusion(bf16[2,3072,2,128]{3,1,2,0:T(8,128)(2,1)} %get-tuple-element.161, s32[]{:T(128)S(6)} %select_n.17, bf16[2,3072,2,128]{3,1,2,0:T(8,128)(2,1)S(1)} %copy-done.4, f32[2,2,512,3072]{3,2,1,0:T(8,128)} %get-tuple-element.149, f32[2,2,512]{2,1,0:T(2,128)S(1)} %get-tuple-element.150, ...), kind=kOutput, calls=%fused_computation.10.clone.1 | convolution fusion | flops 1630011392 | bytes 28852228 | tf_op jit(solution)/shard_map/while/body/eval_jaxpr/nhqk,nkhd->nqhd/dot_general | solution.py:92
  184.0 11.2 %multiply_reduce_fusion.3 = (f32[2,2,512]{2,1,0:T(2,128)S(1)}, f32[2,2,512,3072]{3,2,1,0:T(8,128)}) fusion(bf16[2,3072,2,128]{3,1,2,0:T(8,128)(2,1)S(1)} %get-tuple-element.172, bf16[2,3072,2,128]{3,1,2,0:T(8,128)(2,1)} %get-tuple-element.171, s32[]{:T(128)S(6)} %select_n.17), kind=kOutput, calls=%fused_computation.1.clone.1 | convolution fusion | flops 1623193600 | bytes 28844036 | tf_op jit(solution)/shard_map/while/body/eval_jaxpr/nqhd,nkhd->nhqk/dot_general | solution.py:86
  195.2 11.4 %fusion.58 = f32[2,2,512]{2,1,0:T(2,128)S(1)} fusion(f32[2,2,512,3072]{3,2,1,0:T(8,128)} %get-tuple-element.149, f32[2,2,512]{2,1,0:T(2,128)S(1)} %get-tuple-element.150), kind=kLoop, calls=%fused_computation.2.clone.1 | loop fusion | flops 18872320 | bytes 25182208 | tf_op jit(solution)/shard_map/while/body/eval_jaxpr/reduce_sum | solution.py:91
  206.6 11.3 %fusion.59 = bf16[2,3072,2,128]{3,1,2,0:T(8,128)(2,1)} fusion(bf16[2,3072,2,128]{3,1,2,0:T(8,128)(2,1)} %get-tuple-element.161, s32[]{:T(128)S(6)} %select_n.17, bf16[2,3072,2,128]{3,1,2,0:T(8,128)(2,1)S(1)} %copy-done.4, f32[2,2,512,3072]{3,2,1,0:T(8,128)} %get-tuple-element.149, f32[2,2,512]{2,1,0:T(2,128)S(1)} %get-tuple-element.150, ...), kind=kOutput, calls=%fused_computation.10.clone.1 | convolution fusion | flops 1630011392 | bytes 28852228 | tf_op jit(solution)/shard_map/while/body/eval_jaxpr/nhqk,nkhd->nqhd/dot_general | solution.py:92
  217.9 11.3 %multiply_reduce_fusion.3 = (f32[2,2,512]{2,1,0:T(2,128)S(1)}, f32[2,2,512,3072]{3,2,1,0:T(8,128)}) fusion(bf16[2,3072,2,128]{3,1,2,0:T(8,128)(2,1)S(1)} %get-tuple-element.172, bf16[2,3072,2,128]{3,1,2,0:T(8,128)(2,1)} %get-tuple-element.171, s32[]{:T(128)S(6)} %select_n.17), kind=kOutput, calls=%fused_computation.1.clone.1 | convolution fusion | flops 1623193600 | bytes 28844036 | tf_op jit(solution)/shard_map/while/body/eval_jaxpr/nqhd,nkhd->nhqk/dot_general | solution.py:86
  229.2 11.3 %fusion.58 = f32[2,2,512]{2,1,0:T(2,128)S(1)} fusion(f32[2,2,512,3072]{3,2,1,0:T(8,128)} %get-tuple-element.149, f32[2,2,512]{2,1,0:T(2,128)S(1)} %get-tuple-element.150), kind=kLoop, calls=%fused_computation.2.clone.1 | loop fusion | flops 18872320 | bytes 25182208 | tf_op jit(solution)/shard_map/while/body/eval_jaxpr/reduce_sum | solution.py:91
  240.5 11.1 %fusion.59 = bf16[2,3072,2,128]{3,1,2,0:T(8,128)(2,1)} fusion(bf16[2,3072,2,128]{3,1,2,0:T(8,128)(2,1)} %get-tuple-element.161, s32[]{:T(128)S(6)} %select_n.17, bf16[2,3072,2,128]{3,1,2,0:T(8,128)(2,1)S(1)} %copy-done.4, f32[2,2,512,3072]{3,2,1,0:T(8,128)} %get-tuple-element.149, f32[2,2,512]{2,1,0:T(2,128)S(1)} %get-tuple-element.150, ...), kind=kOutput, calls=%fused_computation.10.clone.1 | convolution fusion | flops 1630011392 | bytes 28852228 | tf_op jit(solution)/shard_map/while/body/eval_jaxpr/nhqk,nkhd->nqhd/dot_general | solution.py:92
  251.6 11.2 %multiply_reduce_fusion.3 = (f32[2,2,512]{2,1,0:T(2,128)S(1)}, f32[2,2,512,3072]{3,2,1,0:T(8,128)}) fusion(bf16[2,3072,2,128]{3,1,2,0:T(8,128)(2,1)S(1)} %get-tuple-element.172, bf16[2,3072,2,128]{3,1,2,0:T(8,128)(2,1)} %get-tuple-element.171, s32[]{:T(128)S(6)} %select_n.17), kind=kOutput, calls=%fused_computation.1.clone.1 | convolution fusion | flops 1623193600 | bytes 28844036 | tf_op jit(solution)/shard_map/while/body/eval_jaxpr/nqhd,nkhd->nhqk/dot_general | solution.py:86
  262.8 11.2 %fusion.58 = f32[2,2,512]{2,1,0:T(2,128)S(1)} fusion(f32[2,2,512,3072]{3,2,1,0:T(8,128)} %get-tuple-element.149, f32[2,2,512]{2,1,0:T(2,128)S(1)} %get-tuple-element.150), kind=kLoop, calls=%fused_computation.2.clone.1 | loop fusion | flops 18872320 | bytes 25182208 | tf_op jit(solution)/shard_map/while/body/eval_jaxpr/reduce_sum | solution.py:91
  274.1 11.1 %fusion.59 = bf16[2,3072,2,128]{3,1,2,0:T(8,128)(2,1)} fusion(bf16[2,3072,2,128]{3,1,2,0:T(8,128)(2,1)} %get-tuple-element.161, s32[]{:T(128)S(6)} %select_n.17, bf16[2,3072,2,128]{3,1,2,0:T(8,128)(2,1)S(1)} %copy-done.4, f32[2,2,512,3072]{3,2,1,0:T(8,128)} %get-tuple-element.149, f32[2,2,512]{2,1,0:T(2,128)S(1)} %get-tuple-element.150, ...), kind=kOutput, calls=%fused_computation.10.clone.1 | convolution fusion | flops 1630011392 | bytes 28852228 | tf_op jit(solution)/shard_map/while/body/eval_jaxpr/nhqk,nkhd->nqhd/dot_general | solution.py:92
  285.2 11.2 %multiply_reduce_fusion.3 = (f32[2,2,512]{2,1,0:T(2,128)S(1)}, f32[2,2,512,3072]{3,2,1,0:T(8,128)}) fusion(bf16[2,3072,2,128]{3,1,2,0:T(8,128)(2,1)S(1)} %get-tuple-element.172, bf16[2,3072,2,128]{3,1,2,0:T(8,128)(2,1)} %get-tuple-element.171, s32[]{:T(128)S(6)} %select_n.17), kind=kOutput, calls=%fused_computation.1.clone.1 | convolution fusion | flops 1623193600 | bytes 28844036 | tf_op jit(solution)/shard_map/while/body/eval_jaxpr/nqhd,nkhd->nhqk/dot_general | solution.py:86
  296.4 11.2 %fusion.58 = f32[2,2,512]{2,1,0:T(2,128)S(1)} fusion(f32[2,2,512,3072]{3,2,1,0:T(8,128)} %get-tuple-element.149, f32[2,2,512]{2,1,0:T(2,128)S(1)} %get-tuple-element.150), kind=kLoop, calls=%fused_computation.2.clone.1 | loop fusion | flops 18872320 | bytes 25182208 | tf_op jit(solution)/shard_map/while/body/eval_jaxpr/reduce_sum | solution.py:91
  307.6 11.1 %fusion.59 = bf16[2,3072,2,128]{3,1,2,0:T(8,128)(2,1)} fusion(bf16[2,3072,2,128]{3,1,2,0:T(8,128)(2,1)} %get-tuple-element.161, s32[]{:T(128)S(6)} %select_n.17, bf16[2,3072,2,128]{3,1,2,0:T(8,128)(2,1)S(1)} %copy-done.4, f32[2,2,512,3072]{3,2,1,0:T(8,128)} %get-tuple-element.149, f32[2,2,512]{2,1,0:T(2,128)S(1)} %get-tuple-element.150, ...), kind=kOutput, calls=%fused_computation.10.clone.1 | convolution fusion | flops 1630011392 | bytes 28852228 | tf_op jit(solution)/shard_map/while/body/eval_jaxpr/nhqk,nkhd->nqhd/dot_general | solution.py:92
  318.7 11.2 %multiply_reduce_fusion.3 = (f32[2,2,512]{2,1,0:T(2,128)S(1)}, f32[2,2,512,3072]{3,2,1,0:T(8,128)}) fusion(bf16[2,3072,2,128]{3,1,2,0:T(8,128)(2,1)S(1)} %get-tuple-element.172, bf16[2,3072,2,128]{3,1,2,0:T(8,128)(2,1)} %get-tuple-element.171, s32[]{:T(128)S(6)} %select_n.17), kind=kOutput, calls=%fused_computation.1.clone.1 | convolution fusion | flops 1623193600 | bytes 28844036 | tf_op jit(solution)/shard_map/while/body/eval_jaxpr/nqhd,nkhd->nhqk/dot_general | solution.py:86
  329.9 11.2 %fusion.58 = f32[2,2,512]{2,1,0:T(2,128)S(1)} fusion(f32[2,2,512,3072]{3,2,1,0:T(8,128)} %get-tuple-element.149, f32[2,2,512]{2,1,0:T(2,128)S(1)} %get-tuple-element.150), kind=kLoop, calls=%fused_computation.2.clone.1 | loop fusion | flops 18872320 | bytes 25182208 | tf_op jit(solution)/shard_map/while/body/eval_jaxpr/reduce_sum | solution.py:91
  341.2 13.9 %fusion.59 = bf16[2,3072,2,128]{3,1,2,0:T(8,128)(2,1)} fusion(bf16[2,3072,2,128]{3,1,2,0:T(8,128)(2,1)} %get-tuple-element.161, s32[]{:T(128)S(6)} %select_n.17, bf16[2,3072,2,128]{3,1,2,0:T(8,128)(2,1)S(1)} %copy-done.4, f32[2,2,512,3072]{3,2,1,0:T(8,128)} %get-tuple-element.149, f32[2,2,512]{2,1,0:T(2,128)S(1)} %get-tuple-element.150, ...), kind=kOutput, calls=%fused_computation.10.clone.1 | convolution fusion | flops 1630011392 | bytes 28852228 | tf_op jit(solution)/shard_map/while/body/eval_jaxpr/nhqk,nkhd->nqhd/dot_general | solution.py:92
  363.5 7.8 %copy.86 = bf16[8,8,12,3072]{3,1,2,0:T(8,128)(2,1)} copy(bf16[8,8,12,3072]{3,2,1,0:T(8,128)(2,1)} %bitcast.22) | data formatting | bytes 9437184 | tf_op jit(solution)/shard_map/all_to_all | solution.py:63
  371.3 30.1 %all-to-all-done.3 = bf16[2,64,48,2,128]{4,2,3,0,1:T(8,128)(2,1)S(1)} async-done(((bf16[2,64,48,2,128]{4,2,3,0,1:T(8,128)(2,1)}), bf16[2,64,48,2,128]{4,2,3,0,1:T(8,128)(2,1)S(1)}, u32[]{:S(2)}, u32[]{:S(2)}) %all-to-all-start.3) | async-done | bytes 3145760 | tf_op jit(solution)/shard_map/all_to_all | solution.py:103
  417.2 211.6 %all-to-all-done.5 = bf16[8,8,12,3072]{3,1,2,0:T(8,128)(2,1)} async-done(((bf16[8,8,12,3072]{3,1,2,0:T(8,128)(2,1)}), bf16[8,8,12,3072]{3,1,2,0:T(8,128)(2,1)}, u32[]{:S(2)}, u32[]{:S(2)}) %all-to-all-start.5) | async-done | bytes 4718624 | tf_op jit(solution)/shard_map/all_to_all | solution.py:62
  628.8 7.7 %copy.87 = bf16[2,8,4,12,3072]{4,3,2,1,0:T(8,128)(2,1)} copy(bf16[2,8,4,12,3072]{4,1,3,0,2:T(8,128)(2,1)} %bitcast.24) | data formatting | bytes 9437184 | tf_op jit(solution)/shard_map/all_to_all | solution.py:62
  636.5 7.5 %reshape.105 = bf16[768,3072]{1,0:T(8,128)(2,1)} reshape(bf16[2,8,4,12,3072]{4,3,2,1,0:T(8,128)(2,1)} %copy.87) | data formatting | bytes 9437184 | tf_op jit(solution)/shard_map/reshape | solution.py:50
  644.0 20.6 %convolution_convert_fusion = bf16[768,3072]{1,0:T(8,128)(2,1)} fusion(bf16[768,3072]{1,0:T(8,128)(2,1)} %reshape.105, bf16[3072,3072]{1,0:T(8,128)(2,1)} %all-gather.5.cloned.1.call-done), kind=kOutput, calls=%fused_computation.23 | convolution fusion | flops 14497873920 | bytes 28311552 | tf_op jit(solution)/shard_map/dot_general | solution.py:51
  664.6 18.9 %fusion.24 = bf16[2,384,3072]{2,1,0:T(8,128)(2,1)} fusion(bf16[2,384,3072]{2,1,0:T(8,128)(2,1)} %bitcast.81, bf16[2,384,3072]{2,1,0:T(8,128)(2,1)} %bitcast.80, bf16[2,384,2048]{2,1,0:T(8,128)(2,1)} %dot_general.29, bf16[2048,3072]{1,0:T(8,128)(2,1)} %all-gather.3.cloned.1.call-done, f32[2,3072]{1,0:T(2,128)S(1)} %constant_dynamic-slice_fusion), kind=kOutput, calls=%fused_computation.18 | convolution fusion | flops 9677832192 | bytes 29908992 | tf_op jit(solution)/shard_map/dot_general | solution.py:155
  (71 shorter events, 86.8 us)
Async XLA Ops:
  6.5 1.9 copy-start
  6.5 637.5 %all-gather.5.cloned.1.call-start = ((), (), s32[]{:S(2)}) async-start(), calls=%async_computation.7 | async-start | bytes 23592960 | tf_op jit(solution)/shard_map/all_gather | solution.py:53
  11.0 43.1 %all-to-all-start.1 = ((bf16[2,8,48,16,128]{4,2,1,0,3:T(8,128)(2,1)}), bf16[2,8,48,16,128]{4,2,1,0,3:T(8,128)(2,1)S(1)}, u32[]{:S(2)}, u32[]{:S(2)}) async-start(bf16[2,8,48,16,128]{4,2,1,0,3:T(8,128)(2,1)} %copy_bitcast_fusion.1), calls=%async_computation.1 | async-start | bytes 6291456 | tf_op jit(solution)/shard_map/all_to_all | solution.py:146
  20.6 38.7 %copy-start.11 = (s32[8]{0:T(128)S(1)}, s32[8]{0:T(128)}, u32[]{:S(2)}) copy-start(s32[8]{0:T(128)} %param.19) | copy-start | bytes 100
  54.0 5.2 copy-start.2
  54.0 42.4 %all-to-all-start.2 = ((bf16[2,8,48,16,128]{4,2,1,0,3:T(8,128)(2,1)}), bf16[2,8,48,16,128]{4,2,1,0,3:T(8,128)(2,1)}, u32[]{:S(2)}, u32[]{:S(2)}) async-start(bf16[2,8,48,16,128]{4,2,1,0,3:T(8,128)(2,1)} %copy_bitcast_fusion), calls=%async_computation.2 | async-start | bytes 6291456 | tf_op jit(solution)/shard_map/all_to_all | solution.py:149
  58.5 606.1 %all-gather.3.cloned.1.call-start = ((), (), s32[]{:S(2)}) async-start(), calls=%async_computation.6 | async-start | bytes 15728640 | tf_op jit(solution)/shard_map/all_gather | solution.py:157
  69.0 10.9 %copy-start.9 = (s32[1,64,12]{1,0,2:T(1,128)S(1)}, s32[1,64,12]{1,0,2:T(1,128)}, u32[]{:S(2)}) copy-start(s32[1,64,12]{1,0,2:T(1,128)} %param.17) | copy-start | bytes 9220
  69.0 11.1 %copy-start.10 = (s32[1,64,12]{1,0,2:T(1,128)S(1)}, s32[1,64,12]{1,0,2:T(1,128)}, u32[]{:S(2)}) copy-start(s32[1,64,12]{1,0,2:T(1,128)} %param.18) | copy-start | bytes 9220
  69.0 11.5 %copy-start.3 = (bf16[2,8,48,2048]{3,2,1,0:T(8,128)(2,1)S(1)}, bf16[2,8,48,2048]{3,2,1,0:T(8,128)(2,1)}, u32[]{:S(2)}) copy-start(bf16[2,8,48,2048]{3,2,1,0:T(8,128)(2,1)} %param.26) | copy-start | bytes 9437188
  80.4 2.7 copy-start.7
  88.2 12.7 %copy-start.5 = (bf16[256,3072]{1,0:T(8,128)(2,1)S(1)}, bf16[256,3072]{1,0:T(8,128)(2,1)}, u32[]{:S(2)}) copy-start(bf16[256,3072]{1,0:T(8,128)(2,1)} %param.21) | copy-start | bytes 4718596
  96.4 42.4 %all-to-all-start = ((bf16[2,8,48,16,128]{4,2,1,0,3:T(8,128)(2,1)}), bf16[2,8,48,16,128]{4,2,1,0,3:T(8,128)(2,1)}, u32[]{:S(2)}, u32[]{:S(2)}) async-start(bf16[2,8,48,16,128]{4,2,1,0,3:T(8,128)(2,1)} %copy_bitcast_fusion.2), calls=%async_computation | async-start | bytes 6291456 | tf_op jit(solution)/shard_map/all_to_all | solution.py:143
  100.9 7.8 %copy-start.6 = (bf16[256,3072]{1,0:T(8,128)(2,1)S(1)}, bf16[256,3072]{1,0:T(8,128)(2,1)}, u32[]{:S(2)}) copy-start(bf16[256,3072]{1,0:T(8,128)(2,1)} %param.22) | copy-start | bytes 4718596
  100.9 8.1 %copy-start.8 = (f32[3072]{0:T(1024)S(1)}, f32[3072]{0:T(1024)}, u32[]{:S(2)}) copy-start(f32[3072]{0:T(1024)} %param.23) | copy-start | bytes 36868
  138.7 220.8 %all-to-all-start.4 = ((bf16[1,64,12,3072]{3,2,0,1:T(8,128)(2,1)}), bf16[1,64,12,3072]{3,2,0,1:T(8,128)(2,1)}, u32[]{:S(2)}, u32[]{:S(2)}) async-start(bf16[1,64,12,3072]{3,2,0,1:T(8,128)(2,1)} %bitcast.73), calls=%async_computation.4 | async-start | bytes 12582912 | tf_op jit(solution)/shard_map/all_to_all | solution.py:63
  161.5 11.3 %copy-start.4 = (bf16[2,3072,2,128]{3,1,2,0:T(8,128)(2,1)S(1)}, bf16[2,3072,2,128]{3,1,2,0:T(8,128)(2,1)}, u32[]{:S(2)}) copy-start(bf16[2,3072,2,128]{3,1,2,0:T(8,128)(2,1)} %get-tuple-element.173) | copy-start | bytes 9437188 | tf_op jit(solution)/shard_map/while
  195.2 11.4 %copy-start.4 = (bf16[2,3072,2,128]{3,1,2,0:T(8,128)(2,1)S(1)}, bf16[2,3072,2,128]{3,1,2,0:T(8,128)(2,1)}, u32[]{:S(2)}) copy-start(bf16[2,3072,2,128]{3,1,2,0:T(8,128)(2,1)} %get-tuple-element.173) | copy-start | bytes 9437188 | tf_op jit(solution)/shard_map/while
  229.2 11.3 %copy-start.4 = (bf16[2,3072,2,128]{3,1,2,0:T(8,128)(2,1)S(1)}, bf16[2,3072,2,128]{3,1,2,0:T(8,128)(2,1)}, u32[]{:S(2)}) copy-start(bf16[2,3072,2,128]{3,1,2,0:T(8,128)(2,1)} %get-tuple-element.173) | copy-start | bytes 9437188 | tf_op jit(solution)/shard_map/while
  262.8 11.2 %copy-start.4 = (bf16[2,3072,2,128]{3,1,2,0:T(8,128)(2,1)S(1)}, bf16[2,3072,2,128]{3,1,2,0:T(8,128)(2,1)}, u32[]{:S(2)}) copy-start(bf16[2,3072,2,128]{3,1,2,0:T(8,128)(2,1)} %get-tuple-element.173) | copy-start | bytes 9437188 | tf_op jit(solution)/shard_map/while
  296.4 11.2 %copy-start.4 = (bf16[2,3072,2,128]{3,1,2,0:T(8,128)(2,1)S(1)}, bf16[2,3072,2,128]{3,1,2,0:T(8,128)(2,1)}, u32[]{:S(2)}) copy-start(bf16[2,3072,2,128]{3,1,2,0:T(8,128)(2,1)} %get-tuple-element.173) | copy-start | bytes 9437188 | tf_op jit(solution)/shard_map/while
  329.9 11.2 %copy-start.4 = (bf16[2,3072,2,128]{3,1,2,0:T(8,128)(2,1)S(1)}, bf16[2,3072,2,128]{3,1,2,0:T(8,128)(2,1)}, u32[]{:S(2)}) copy-start(bf16[2,3072,2,128]{3,1,2,0:T(8,128)(2,1)} %get-tuple-element.173) | copy-start | bytes 9437188 | tf_op jit(solution)/shard_map/while
  359.5 41.8 %all-to-all-start.3 = ((bf16[2,64,48,2,128]{4,2,3,0,1:T(8,128)(2,1)}), bf16[2,64,48,2,128]{4,2,3,0,1:T(8,128)(2,1)S(1)}, u32[]{:S(2)}, u32[]{:S(2)}) async-start(bf16[2,64,48,2,128]{4,2,3,0,1:T(8,128)(2,1)} %copy.78), calls=%async_computation.3 | async-start | bytes 6291456 | tf_op jit(solution)/shard_map/all_to_all | solution.py:103
  401.4 227.5 %all-to-all-start.5 = ((bf16[8,8,12,3072]{3,1,2,0:T(8,128)(2,1)}), bf16[8,8,12,3072]{3,1,2,0:T(8,128)(2,1)}, u32[]{:S(2)}, u32[]{:S(2)}) async-start(bf16[8,8,12,3072]{3,1,2,0:T(8,128)(2,1)} %copy.86), calls=%async_computation.5 | async-start | bytes 9437184 | tf_op jit(solution)/shard_map/all_to_all | solution.py:62
  664.6 18.9 %copy-start.1 = (bf16[2,8,48,2048]{3,2,1,0:T(8,128)(2,1)S(1)}, bf16[2,8,48,2048]{3,2,1,0:T(8,128)(2,1)}, u32[]{:S(2)}) copy-start(bf16[2,8,48,2048]{3,2,1,0:T(8,128)(2,1)} %param.27) | copy-start | bytes 9437188
Sparse Core Ops, SparseCore 0:
  8.9 325.2 all-gather.4
  335.8 317.8 all-gather.2
where the time goes:
time: 692 us; the launch traced here: 690 us
  waiting for transfers between devices  296 us (43%)
  matrix products  190 us (27%)
  local copies, waits for them, and re-layouts  91.3 us (13%)
  other arithmetic  71.9 us (10%)
  starting transfers between devices  28.2 us (4%)
  between operations  13.6 us (2%)
    all_to_all x1, waiting for transfers between devices, relayout(): lax.all_to_all(lax.all_to_all(field, 'seq', split_axis=1, concat_axis=0,...  212 us
    dot_general x6, matrix products, one_block(): jnp.einsum('nhqk,nkhd->nqhd', weights.astype(jnp.bfloat16), values_all, p...  69.7 us
    reduce_sum x6, other arithmetic, one_block(): totals = jnp.sum(weights, axis=3)  67.7 us
    dot_general x6, matrix products, one_block(): jnp.einsum('nqhd,nkhd->nhqk', query_block, keys_all, preferred_element_ty...  67.3 us
    all_to_all x1, waiting for transfers between devices, per_device(): lax.all_to_all(key.reshape(split_shape), 'seq', split_axis=3, concat_axis...  33.4 us
    all_to_all x1, waiting for transfers between devices, attend(): lax.all_to_all(output, 'seq', split_axis=1, concat_axis=3, tiled=True)  30.1 us
    convert_element_type x2, local copies, waits for them, and re-layouts, condition(): control_hidden_state.reshape(-1, feature_width).astype(jnp.float32)  20.7 us
    dot_general x1, matrix products, project(): jnp.dot(flattened, lax.all_gather(control_output_weight, 'ctl', axis=0, t...  20.6 us
  transfers between devices with their start and end apart: 8, of which 5 were waited for; matrix products, arithmetic and copies ran while one was open for 48% of the time, Pallas kernels for 0%

commit v1 on v0

v1 whole, which is shorter than its diff:
```python
import functools
import math

import jax
import jax.numpy as jnp
from jax import lax
from jax.experimental import pallas as pl
from jax.experimental.pallas import tpu as pltpu
from jax.sharding import PartitionSpec as P

HEAD_DIM = 128
MESH = pl.DeviceIdType.MESH
F32 = jnp.float32
BF16 = jnp.bfloat16


def time_embed(timestep, timestep_weight):
    half = timestep_weight.shape[0] // 2
    freqs = jnp.exp(-math.log(10000.0) * jnp.arange(half, dtype=F32) / half)
    angles = timestep.astype(F32)[:, None] * freqs[None, :]
    features = jnp.concatenate([jnp.cos(angles), jnp.sin(angles)], axis=1).astype(BF16)
    return jax.nn.silu(jnp.dot(features, timestep_weight, preferred_element_type=F32))


def condition_kernel(depth_base, x_ref, seg_ref, dep_ref, table_ref, gain_ref, o_ref, rows_ref):
    grid_rows, grid_cols = x_ref.shape[1], x_ref.shape[2]
    for r in range(grid_rows):
        rows_ref[r * grid_cols : (r + 1) * grid_cols, :] = x_ref[0, r].astype(F32)
    tokens, classes = rows_ref.shape[0], table_ref.shape[0]
    iota = lax.broadcasted_iota(jnp.int32, (tokens, classes), 1)
    hit = jnp.logical_or(iota == seg_ref[0], iota == dep_ref[0] + depth_base)
    onehot = jnp.where(hit, 1.0, 0.0).astype(BF16)
    mixed = rows_ref[...] + jnp.dot(onehot, table_ref[...], preferred_element_type=F32)
    scale = lax.rsqrt(jnp.mean(mixed * mixed, axis=-1, keepdims=True) + 1e-06)
    o_ref[0] = (mixed * scale * gain_ref[0]).astype(BF16)


def condition(hidden, seg, dep, seg_table, dep_table, gain_rows, groups):
    images, rows, cols, width = hidden.shape
    part = rows // groups
    tokens = part * cols
    depth_base = -(-seg_table.shape[0] // 256) * 256
    table = jnp.concatenate(
        [jnp.pad(seg_table, ((0, depth_base - seg_table.shape[0]), (0, 0))), dep_table], axis=0
    )
    column = pl.BlockSpec((1, tokens, 1), lambda b, r: (b, r, 0))
    return pl.pallas_call(
        functools.partial(condition_kernel, depth_base),
        out_shape=jax.ShapeDtypeStruct((images, rows * cols, width), BF16),
        grid=(images, groups),
        in_specs=[
            pl.BlockSpec((1, part, cols, width), lambda b, r: (b, r, 0, 0)),
            column,
            column,
            pl.BlockSpec(table.shape, lambda b, r: (0, 0)),
            pl.BlockSpec((1, 1, width), lambda b, r: (b, 0, 0)),
        ],
        out_specs=pl.BlockSpec((1, tokens, width), lambda b, r: (b, r, 0)),
        scratch_shapes=[pltpu.VMEM((tokens, width), F32)],
        compiler_params=pltpu.CompilerParams(vmem_limit_bytes=48 * 2**20),
    )(
        hidden,
        seg.reshape(images, rows * cols, 1),
        dep.reshape(images, rows * cols, 1),
        table,
        gain_rows[:, None, :],
    )


def exchange_kernel(
    n_ctl, n_seq,
    q_ref, k_ref, v_ref, c_ref, wc_ref, wa_ref,
    att_ref, c1_ref, c2_ref, wcf_ref, waf_ref,
    qb, kb, vb, vx, ob,
    qkv_s, qkv_r, o_s, o_r, c1_s, c1_r, c2_s, c2_r,
    wz_s, wz_r, wp_s, wp_r, wf_s, wf_r, az_s, az_r, af_s, af_r, loc,
):
    z, s = lax.axis_index("ctl"), lax.axis_index("seq")
    core = lax.rem(s, 2)
    sib = s + 1 - 2 * core
    seq_peers = [lax.rem(s + i, n_seq) for i in range(1, n_seq)]
    ctl_peers = [lax.rem(z + i, n_ctl) for i in range(1, n_ctl)]

    barrier = pltpu.get_barrier_semaphore()
    for p in seq_peers:
        pl.semaphore_signal(barrier, inc=1, device_id=(z, p), device_id_type=MESH)
    for p in ctl_peers:
        pl.semaphore_signal(barrier, inc=1, device_id=(p, s), device_id_type=MESH)
    pl.semaphore_wait(barrier, n_seq + n_ctl - 2)

    images, own_tokens, inner = q_ref.shape
    length = own_tokens * n_seq
    hw = inner // n_seq
    heads = hw // HEAD_DIM

    def rem(src, dst, ss, rs, dz, ds):
        return pltpu.make_async_remote_copy(
            src_ref=src, dst_ref=dst, send_sem=ss, recv_sem=rs,
            device_id=(dz, ds), device_id_type=MESH,
        )

    def aligned(i, n):
        return pl.ds(pl.multiple_of(i * n, n), n)

    wc_rows = wc_ref.shape[0] // n_seq
    wc_mine = wc_ref.at[aligned(s, wc_rows)]
    wa_half = wa_ref.shape[0] // 2
    wa_mine = wa_ref.at[aligned(core, wa_half)]

    wz = [rem(wc_mine, wcf_ref.at[z, s], wz_s.at[i], wz_r.at[i], p, s) for i, p in enumerate(ctl_peers)]
    az = [rem(wa_mine, waf_ref.at[z, core], az_s.at[i], az_r.at[i], p, s) for i, p in enumerate(ctl_peers)]

    own_images, ctl_rows, _ = c_ref.shape
    ct = ctl_rows // n_seq
    c1 = [
        rem(c_ref.at[:, aligned(p, ct), :], c1_ref.at[pl.ds(s * own_images, own_images)],
            c1_s.at[i], c1_r.at[i], z, p)
        for i, p in enumerate(seq_peers)
    ]
    qkv = [
        [
            rem(src.at[g, :, aligned(p, hw)], dst.at[g, aligned(s, own_tokens), :],
                qkv_s.at[g, a, i], qkv_r.at[g, a, i], z, p)
            for a, (src, dst) in enumerate(((q_ref, qb), (k_ref, kb), (v_ref, vb)))
            for i, p in enumerate(seq_peers)
        ]
        for g in range(images)
    ]
    local = [
        pltpu.make_async_copy(wc_mine, wcf_ref.at[z, s], loc.at[0]),
        pltpu.make_async_copy(wa_ref.at[aligned(0, wa_half)], waf_ref.at[z, 0], loc.at[1]),
        pltpu.make_async_copy(wa_ref.at[aligned(1, wa_half)], waf_ref.at[z, 1], loc.at[2]),
        pltpu.make_async_copy(
            c_ref.at[:, aligned(s, ct), :], c1_ref.at[pl.ds(s * own_images, own_images)], loc.at[3]),
    ]
    mine = [
        pltpu.make_async_copy(
            src.at[g, :, aligned(s, hw)], dst.at[g, aligned(s, own_tokens), :], loc.at[4 + 3 * g + a])
        for g in range(images)
        for a, (src, dst) in enumerate(((q_ref, qb), (k_ref, kb), (v_ref, vb)))
    ]

    for c in wz + c1 + qkv[0]:
        c.start()
    for c in local + mine:
        c.start()
    for g in range(1, images):
        for c in qkv[g]:
            c.start()
    for c in az:
        c.start()

    for c in c1:
        c.wait_recv()
    local[3].wait()
    pair = c1_ref.shape[0] // n_ctl
    c2 = [
        rem(c1_ref.at[pl.ds(p * pair, pair)], c2_ref.at[z], c2_s.at[i], c2_r.at[i], p, s)
        for i, p in enumerate(ctl_peers)
    ]
    for c in c2:
        c.start()
    c2_own = pltpu.make_async_copy(
        c1_ref.at[pl.ds(z * pair, pair)], c2_ref.at[z], loc.at[4 + 3 * images])
    c2_own.start()

    for c in wz:
        c.wait_recv()
    local[0].wait()
    chip_peers = [lax.rem(s + 2 * j, n_seq) for j in range(1, n_seq // 2)]
    wp = [
        rem(wcf_ref.at[:, s], wcf_ref.at[:, s], wp_s.at[i], wp_r.at[i], z, p)
        for i, p in enumerate(chip_peers)
    ]
    for c in wp:
        c.start()
    wf = [rem(wcf_ref.at[:, s], wcf_ref.at[:, s], wf_s.at[0], wf_r.at[0], z, sib)]
    wf[0].start()

    scale = HEAD_DIM ** (-0.5) * math.log2(math.e)
    block = math.gcd(length, 256)
    o_copies = []
    for g in range(images):
        for c in qkv[g]:
            c.wait_recv()
        for a in range(3):
            mine[3 * g + a].wait()
        for h in range(heads):
            vx[h, :, 0:HEAD_DIM] = vb[g, :, h * HEAD_DIM : (h + 1) * HEAD_DIM]
            if g == 0:
                vx[h, :, HEAD_DIM : 2 * HEAD_DIM] = jnp.ones((length, HEAD_DIM), BF16)

        @pl.loop(0, length // block)
        def _(j):
            rows = pl.ds(pl.multiple_of(j * block, block), block)
            for h in range(heads):
                cols = slice(h * HEAD_DIM, (h + 1) * HEAD_DIM)
                scores = lax.dot_general(
                    qb[g, rows, cols], kb[g, :, cols], (((1,), (1,)), ((), ())),
                    preferred_element_type=F32,
                )
                peak = jnp.max(scores, axis=1, keepdims=True)
                weights = jnp.exp2((scores - peak) * scale).astype(BF16)
                mixed = jnp.dot(weights, vx[h], preferred_element_type=F32)
                ob[g, rows, cols] = (mixed[:, :HEAD_DIM] / mixed[:, HEAD_DIM:]).astype(BF16)

        for i, p in enumerate(seq_peers):
            c = rem(ob.at[g, aligned(p, own_tokens), :], att_ref.at[g, :, aligned(s, hw)],
                    o_s.at[g, i], o_r.at[g, i], z, p)
            c.start()
            o_copies.append(c)
        c = pltpu.make_async_copy(
            ob.at[g, aligned(s, own_tokens), :], att_ref.at[g, :, aligned(s, hw)],
            loc.at[5 + 3 * images + g])
        c.start()
        mine.append(c)

    for j in range(1, n_seq // 2):
        wp[j - 1].wait_recv()
        origin = lax.rem(s + n_seq - 2 * j, n_seq)
        c = rem(wcf_ref.at[:, origin], wcf_ref.at[:, origin], wf_s.at[j], wf_r.at[j], z, sib)
        c.start()
        wf.append(c)
    af = []
    for i in range(1, n_ctl):
        az[i - 1].wait_recv()
        origin = lax.rem(z + n_ctl - i, n_ctl)
        c = rem(waf_ref.at[origin, core], waf_ref.at[origin, core], af_s.at[i - 1], af_r.at[i - 1], z, sib)
        c.start()
        af.append(c)

    for c in c2 + o_copies + wf + af:
        c.wait_recv()
    local[1].wait()
    local[2].wait()
    c2_own.wait()
    for c in mine[3 * images :]:
        c.wait()
    for c in wz + az + c1 + c2 + wp + wf + af + o_copies:
        c.wait_send()
    for g in range(images):
        for c in qkv[g]:
            c.wait_send()


def exchange(q, k, v, normed, wc, wa, n_ctl, n_seq):
    images, own_tokens, inner = q.shape
    length = own_tokens * n_seq
    hw = inner // n_seq
    own_images, ctl_rows, width = normed.shape
    ct = ctl_rows // n_seq
    total = own_images * n_seq
    dma = lambda *shape: pltpu.SemaphoreType.DMA(shape)
    anywhere = pl.BlockSpec(memory_space=pl.ANY)
    flops = 4 * images * length * length * hw
    return pl.pallas_call(
        functools.partial(exchange_kernel, n_ctl, n_seq),
        out_shape=[
            jax.ShapeDtypeStruct(q.shape, BF16),
            jax.ShapeDtypeStruct((total, ct, width), BF16),
            jax.ShapeDtypeStruct((n_ctl, total // n_ctl, ct, width), BF16),
            jax.ShapeDtypeStruct((n_ctl, n_seq, wc.shape[0] // n_seq, wc.shape[1]), BF16),
            jax.ShapeDtypeStruct((n_ctl, 2, wa.shape[0] // 2, wa.shape[1]), BF16),
        ],
        in_specs=[anywhere] * 6,
        out_specs=[anywhere] * 5,
        scratch_shapes=[
            pltpu.VMEM((images, length, hw), BF16),
            pltpu.VMEM((images, length, hw), BF16),
            pltpu.VMEM((images, length, hw), BF16),
            pltpu.VMEM((hw // HEAD_DIM, length, 2 * HEAD_DIM), BF16),
            pltpu.VMEM((images, length, hw), BF16),
            dma(images, 3, n_seq - 1), dma(images, 3, n_seq - 1),
            dma(images, n_seq - 1), dma(images, n_seq - 1),
            dma(n_seq - 1), dma(n_seq - 1),
            dma(n_ctl - 1), dma(n_ctl - 1),
            dma(n_ctl - 1), dma(n_ctl - 1),
            dma(n_seq // 2 - 1), dma(n_seq // 2 - 1),
            dma(n_seq // 2), dma(n_seq // 2),
            dma(n_ctl - 1), dma(n_ctl - 1),
            dma(n_ctl - 1), dma(n_ctl - 1),
            dma(5 + 4 * images),
        ],
        compiler_params=pltpu.CompilerParams(
            collective_id=0, has_side_effects=True, vmem_limit_bytes=52 * 2**20
        ),
        cost_estimate=pl.CostEstimate(
            flops=flops, bytes_accessed=64 * 2**20, transcendentals=images * length * length * 2
        ),
    )(q, k, v, normed, wc, wa)


def per_device(
    n_ctl, n_seq,
    control_hidden_state,
    patch_segment_labels,
    patch_depth_levels,
    timestep,
    segment_label_embedding,
    depth_level_embedding,
    timestep_weight,
    control_norm_gain,
    control_output_weight,
    transformer_hidden_state,
    query,
    key,
    value,
    attention_output_weight,
):
    gain = time_embed(timestep, timestep_weight)
    own_images, _, ctl_cols, width = control_hidden_state.shape
    ctl_gain = lax.dynamic_slice_in_dim(gain, lax.axis_index("seq") * own_images, own_images, 0)
    normed = condition(
        control_hidden_state,
        patch_segment_labels,
        patch_depth_levels,
        segment_label_embedding,
        depth_level_embedding,
        control_norm_gain * (1.0 + ctl_gain),
        n_seq,
    )
    images, rows, cols, inner = query.shape
    tokens = rows * cols
    flat = lambda a: a.reshape(images, tokens, inner)
    attended, _, arrived, wc_full, wa_full = exchange(
        flat(query), flat(key), flat(value), normed,
        control_output_weight, attention_output_weight, n_ctl, n_seq,
    )
    out_index = jnp.arange(images * tokens, dtype=jnp.int32)
    image, place = out_index // tokens, out_index % tokens
    row, col = place // cols, place % cols
    source = (
        ((col // ctl_cols) * images + image) * (rows * ctl_cols) + row * ctl_cols + col % ctl_cols
    )
    order = (source[:, None] == out_index[None, :]).astype(BF16)
    normed_rows = jnp.dot(
        order, arrived.reshape(images * tokens, width), preferred_element_type=F32
    ).astype(BF16)
    residual = jnp.dot(
        normed_rows, wc_full.reshape(-1, width), preferred_element_type=F32
    ).astype(BF16)
    projected = jnp.dot(
        attended.reshape(images * tokens, inner),
        wa_full.reshape(inner, width),
        preferred_element_type=F32,
    )
    t_gain = lax.dynamic_slice_in_dim(gain, lax.axis_index("ctl") * images, images, 0)
    shape = (images, tokens, width)
    final = (
        transformer_hidden_state.reshape(shape).astype(F32)
        + t_gain[:, None, :] * projected.reshape(shape)
        + residual.reshape(shape).astype(F32)
    )
    return final.astype(BF16).reshape(transformer_hidden_state.shape)


def solution(mesh):
    return jax.shard_map(
        functools.partial(per_device, mesh.shape["ctl"], mesh.shape["seq"]),
        mesh=mesh,
        in_specs=(
            P("seq", None, "ctl", None),
            P("seq", None, "ctl"),
            P("seq", None, "ctl"),
            P(),
            P(),
            P(),
            P(),
            P(),
            P("ctl", None),
            P("ctl", "seq", None, None),
            P("ctl", "seq", None, None),
            P("ctl", "seq", None, None),
            P("ctl", "seq", None, None),
            P("ctl", None),
        ),
        out_specs=P("ctl", "seq", None, None),
        check_vma=False,
    )
```

time: 692 us -> 366 us (0.53)
  Pallas kernels: 0 us -> 304 us
  waiting for transfers between devices: 296 us -> 0 us
  matrix products: 190 us -> 47.3 us
  local copies, waits for them, and re-layouts: 91.3 us -> 8.05 us
  other arithmetic: 71.9 us -> 3.89 us
  starting transfers between devices: 28.2 us -> 0 us
  between operations: 13.6 us -> 0.07 us
    pallas_call x0 -> x2, Pallas kernels: none -> 304 us  [the longest x1 294 us: exchange(): pl.pallas_call(functools.partial(exchange_kernel, n_ctl, n_seq), out_shap...]
    all_to_all x6 -> x0, waiting for transfers between devices: 294 us -> none  [the longest x1 212 us: relayout(): lax.all_to_all(lax.all_to_all(field, 'seq', split_axis=1, concat_axis=0,...]
    dot_general x17 -> x3, matrix products: 190 us -> 47.3 us  [the longest x1 28.4 us: per_device(): jnp.dot(normed_rows, wc_full.reshape(-1, width), preferred_element_type=F32)]
    reduce_sum x6 -> x0, other arithmetic: 67.7 us -> none  [one_block(): totals = jnp.sum(weights, axis=3)]
    all_to_all x6 -> x0, local copies, waits for them, and re-layouts: 31.8 us -> none  [the longest x1 7.8 us: relayout(): lax.all_to_all(field, 'seq', split_axis=1, concat_axis=0, tiled=True)]
    reshape x6 -> x2, local copies, waits for them, and re-layouts: 28.9 us -> 0.31 us  [the longest x1 0.16 us: condition(): dep.reshape(images, rows * cols, 1)]
    all_to_all x6 -> x0, starting transfers between devices: 28.1 us -> none  [the longest x1 5.17 us: per_device(): lax.all_to_all(key.reshape(split_shape), 'seq', split_axis=3, concat_axis...]
    convert_element_type x2 -> x0, local copies, waits for them, and re-layouts: 20.7 us -> none  [condition(): control_hidden_state.reshape(-1, feature_width).astype(jnp.float32)]
  transfers between devices with their start and end apart: 8 -> 0, of which waited for: 5 -> 0; matrix products, arithmetic and copies ran while one was open for 48% -> 0% of each run, Pallas kernels for 0% -> 0%
where the time goes in v1:
time: 366 us; the launch traced here: 364 us
  Pallas kernels  304 us (83%)
  matrix products  47.3 us (13%)
  local copies, waits for them, and re-layouts  8.05 us (2%)
  other arithmetic  3.89 us (1%)
    pallas_call x1, Pallas kernels, exchange(): pl.pallas_call(functools.partial(exchange_kernel, n_ctl, n_seq), out_shap...  294 us
    dot_general x1, matrix products, per_device(): jnp.dot(normed_rows, wc_full.reshape(-1, width), preferred_element_type=F32)  28.4 us
    dot_general x1, matrix products, per_device(): jnp.dot(attended.reshape(images * tokens, inner), wa_full.reshape(inner,...  18.6 us
    pallas_call x1, Pallas kernels, condition(): pl.pallas_call(functools.partial(condition_kernel, depth_base), out_shape...  10.7 us
    unnamed x9, local copies, waits for them, and re-layouts  7.72 us

profile of v1, /device:TPU:0, one launch (start us, length us, event | category | flops | bytes accessed | tf_op | source)
XLA Modules:
  0.0 363.8 jit_solution(13277905824143212616)
XLA Ops:
  0.0 0.0 copy-start
  0.0 0.8 convert_element_type.30
  0.8 0.1 fusion.15
  0.9 0.8 copy.18
  1.7 0.8 copy.19
  2.5 0.0 copy-done
  2.5 0.3 divide_multiply_fusion
  2.8 0.7 multiply_bitcast_fusion.gain_ref
  3.6 0.2 reshape.104.dep_ref
  3.8 0.2 reshape.103.seg_ref
  3.9 0.0 copy-start.2
  3.9 2.2 fusion.2.table_ref
  6.2 0.8 copy-done.2
  7.0 5.3 %copy.20.x_ref = bf16[1,64,12,3072]{3,2,1,0:T(8,128)(2,1)} copy(bf16[1,64,12,3072]{3,1,2,0:T(8,128)(2,1)S(1)} %copy-done.2) | data formatting | bytes 9437184 | tf_op args[0]
  12.3 10.7 %shard_map.136.c_ref = bf16[1,768,3072]{2,1,0:T(8,128)(2,1)} custom-call(bf16[1,64,12,3072]{3,2,1,0:T(8,128)(2,1)} %copy.20.x_ref, s32[1,768,1]{2,1,0:T(8,128)S(1)} %reshape.103.seg_ref, s32[1,768,1]{2,1,0:T(8,128)S(1)} %reshape.104.dep_ref, bf16[512,3072]{1,0:T(8,128)(2,1)S(1)} %fusion.2.table_ref, f32[1,1,3072]{2,1,0:T(1,128)S(1)} %multiply_bitcast_fusion.gain_ref), custom_call_target="tpu_custom_call" | custom-call | tf_op jit(solution)/shard_map/pallas_call | solution.py:47
  23.0 293.8 %shard_map.137 = (bf16[2,384,2048]{2,1,0:T(8,128)(2,1)}, bf16[8,96,3072]{2,1,0:T(8,128)(2,1)}, bf16[4,2,96,3072]{3,2,1,0:T(8,128)(2,1)}, bf16[4,8,96,3072]{3,2,1,0:T(8,128)(2,1)}, bf16[4,2,256,3072]{3,2,1,0:T(8,128)(2,1)}) custom-call(bf16[2,384,2048]{2,1,0:T(8,128)(2,1)} %bitcast.23, bf16[2,384,2048]{2,1,0:T(8,128)(2,1)} %bitcast.24, ...), custom_call_target="tpu_custom_call" | custom-call | flops 19327352832 | bytes 67108864 | tf_op jit(solution)/shard_map/pallas_call | solution.py:256
  316.8 28.4 %convolution_convert_fusion = bf16[768,3072]{1,0:T(8,128)(2,1)} fusion(bf16[3072,3072]{1,0:T(8,128)(2,1)} %bitcast.26, bf16[768,3072]{1,0:T(8,128)(2,1)} %bitcast.28, s32[768]{0:T(1024)S(1)} %fusion.14), kind=kOutput, calls=%fused_computation.5 | convolution fusion | flops 18124701696 | bytes 28314624 | tf_op jit(solution)/shard_map/dot_general | solution.py:339
  345.2 0.0 copy-start.1
  345.2 18.6 %fusion = bf16[2,384,3072]{2,1,0:T(8,128)(2,1)} fusion(bf16[2,384,3072]{2,1,0:T(8,128)(2,1)} %bitcast.29, bf16[2,384,3072]{2,1,0:T(8,128)(2,1)} %bitcast.22, bf16[2,384,2048]{2,1,0:T(8,128)(2,1)} %get-tuple-element.9, bf16[2048,3072,1]{1,0,2:T(8,128)(2,1)} %bitcast.27, f32[2,3072]{1,0:T(2,128)S(1)} %constant_dynamic-slice_fusion), kind=kOutput, calls=%fused_computation.1 | convolution fusion | flops 9677832192 | bytes 29908992 | tf_op jit(solution)/shard_map/dot_general | solution.py:342
  363.8 0.0 copy-done.1
  (3 shorter events, 0.1 us)
Async XLA Ops:
  0.0 2.5 copy-start
  3.9 3.1 copy-start.2
  345.2 18.6 %copy-start.1 = (bf16[256,3072]{1,0:T(8,128)(2,1)S(1)}, bf16[256,3072]{1,0:T(8,128)(2,1)}, u32[]{:S(2)}) copy-start(bf16[256,3072]{1,0:T(8,128)(2,1)} %param.20) | copy-start | bytes 4718596

commit v2 on v1

v2 whole, which is shorter than its diff:
```python
import functools
import math

import jax
import jax.numpy as jnp
from jax import lax
from jax.experimental import pallas as pl
from jax.experimental.pallas import tpu as pltpu
from jax.sharding import PartitionSpec as P

HEAD_DIM = 128
MESH = pl.DeviceIdType.MESH
F32 = jnp.float32
BF16 = jnp.bfloat16


def time_embed(timestep, timestep_weight):
    half = timestep_weight.shape[0] // 2
    freqs = jnp.exp(-math.log(10000.0) * jnp.arange(half, dtype=F32) / half)
    angles = timestep.astype(F32)[:, None] * freqs[None, :]
    features = jnp.concatenate([jnp.cos(angles), jnp.sin(angles)], axis=1).astype(BF16)
    return jax.nn.silu(jnp.dot(features, timestep_weight, preferred_element_type=F32))


def exchange_kernel(
    n_ctl, n_seq, depth_base,
    q_ref, k_ref, v_ref, x_ref, wc_ref, wa_ref, seg_ref, dep_ref, table_ref, gain_ref, order_ref,
    att_ref, res_ref, c1_ref, wcf_ref, waf_ref,
    qb, kb, vb, vx, ob, xb, rows_f, nrm, xr, wb,
    qkv_s, qkv_r, o_s, o_r, c1_s, c1_r, c2_s, c2_r,
    wz_s, wz_r, wp_s, wp_r, wr_s, wr_r, wf_s, wf_r, az_s, az_r, af_s, af_r, loc, xs, ws,
):
    z, s = lax.axis_index("ctl"), lax.axis_index("seq")
    core = lax.rem(s, 2)
    sib = s + 1 - 2 * core
    seq_peers = [lax.rem(s + i, n_seq) for i in range(1, n_seq)]
    ctl_peers = [lax.rem(z + i, n_ctl) for i in range(1, n_ctl)]

    barrier = pltpu.get_barrier_semaphore()
    for p in seq_peers:
        pl.semaphore_signal(barrier, inc=1, device_id=(z, p), device_id_type=MESH)
    for p in ctl_peers:
        pl.semaphore_signal(barrier, inc=1, device_id=(p, s), device_id_type=MESH)
    pl.semaphore_wait(barrier, n_seq + n_ctl - 2)

    images, own_tokens, inner = q_ref.shape
    length = own_tokens * n_seq
    hw = inner // n_seq
    heads = hw // HEAD_DIM
    width = x_ref.shape[3]

    def rem(src, dst, ss, rs, dz, ds):
        return pltpu.make_async_remote_copy(
            src_ref=src, dst_ref=dst, send_sem=ss, recv_sem=rs,
            device_id=(dz, ds), device_id_type=MESH,
        )

    def aligned(i, n):
        return pl.ds(pl.multiple_of(i * n, n), n)

    wc_rows = wc_ref.shape[0] // n_seq
    wc_mine = wc_ref.at[aligned(s, wc_rows)]
    wa_half = wa_ref.shape[0] // 2
    wa_mine = wa_ref.at[aligned(core, wa_half)]
    wz = [rem(wc_mine, wcf_ref.at[z, s], wz_s.at[i], wz_r.at[i], p, s) for i, p in enumerate(ctl_peers)]

    def az(way, step, act):
        step_z = 1 - 2 * way
        origin = z - step_z * (step - 1)
        to = z + step_z
        source_ok = jnp.logical_and(origin >= 0, origin < n_ctl)
        ok = jnp.logical_and(source_ok, jnp.logical_and(to >= 0, to < n_ctl))

        @pl.when(ok)
        def _():
            src = wa_mine if step == 1 else waf_ref.at[origin, core]
            c = rem(src, waf_ref.at[origin, core], az_s.at[way, step - 1], az_r.at[way, step - 1], to, s)
            if act == "start":
                c.start()
            else:
                c.wait_send()

    def az_arrived(way, step, act):
        origin = z - (1 - 2 * way) * step

        @pl.when(jnp.logical_and(origin >= 0, origin < n_ctl))
        def _():
            ref = waf_ref.at[origin, core]
            if act == "wait":
                rem(ref, ref, az_s.at[way, step - 1], az_r.at[way, step - 1], z, sib).wait_recv()
                return
            c = rem(ref, ref, af_s.at[way, step - 1], af_r.at[way, step - 1], z, sib)
            if act == "pass":
                c.start()
            elif act == "passed":
                c.wait_recv()
            else:
                c.wait_send()

    def both(f, step, act):
        for way in range(2):
            f(way, step, act)

    qkv = [
        [
            rem(src.at[g, :, aligned(p, hw)], dst.at[g, aligned(s, own_tokens), :],
                qkv_s.at[g, a, i], qkv_r.at[g, a, i], z, p)
            for a, (src, dst) in enumerate(((q_ref, qb), (k_ref, kb), (v_ref, vb)))
            for i, p in enumerate(seq_peers)
        ]
        for g in range(images)
    ]
    local = [
        pltpu.make_async_copy(wc_mine, wcf_ref.at[z, s], loc.at[0]),
        pltpu.make_async_copy(wa_ref.at[aligned(0, wa_half)], waf_ref.at[z, 0], loc.at[1]),
        pltpu.make_async_copy(wa_ref.at[aligned(1, wa_half)], waf_ref.at[z, 1], loc.at[2]),
    ]
    mine = [
        pltpu.make_async_copy(
            src.at[g, :, aligned(s, hw)], dst.at[g, aligned(s, own_tokens), :], loc.at[4 + 3 * g + a])
        for g in range(images)
        for a, (src, dst) in enumerate(((q_ref, qb), (k_ref, kb), (v_ref, vb)))
    ]

    for c in wz + qkv[0]:
        c.start()
    both(az, 1, "start")

    own_images, grid_rows, grid_cols = x_ref.shape[0], x_ref.shape[1], x_ref.shape[2]
    part = grid_rows // n_seq
    ct = part * grid_cols
    groups = own_images * n_seq

    def x_copy(t, slot):
        return pltpu.make_async_copy(
            x_ref.at[t // n_seq, pl.ds(lax.rem(t, n_seq) * part, part)], xb.at[slot], xs.at[slot])

    x_copy(0, 0).start()
    for c in local + mine:
        c.start()

    @pl.loop(0, groups)
    def _(t):
        slot = lax.rem(t, 2)

        @pl.when(t + 1 < groups)
        def _():
            x_copy(t + 1, 1 - slot).start()

        x_copy(t, slot).wait()
        for r in range(part):
            rows_f[r * grid_cols : (r + 1) * grid_cols, :] = xb[slot, r].astype(F32)
        iota = lax.broadcasted_iota(jnp.int32, (ct, table_ref.shape[0]), 1)
        hit = jnp.logical_or(iota == seg_ref[t], iota == dep_ref[t] + depth_base)
        onehot = jnp.where(hit, 1.0, 0.0).astype(BF16)
        mixed = rows_f[...] + jnp.dot(onehot, table_ref[...], preferred_element_type=F32)
        norm = lax.rsqrt(jnp.mean(mixed * mixed, axis=-1, keepdims=True) + 1e-06)
        nrm[t] = (mixed * norm * gain_ref[t // n_seq]).astype(BF16)

    c1 = [
        [
            rem(nrm.at[b * n_seq + p], c1_ref.at[s * own_images + b], c1_s.at[b, i], c1_r.at[b, i], z, p)
            for i, p in enumerate(seq_peers)
        ]
        for b in range(own_images)
    ]
    c1 = [c for each in c1 for c in each]
    c1_own = [
        pltpu.make_async_copy(nrm.at[b * n_seq + s], c1_ref.at[s * own_images + b], loc.at[5 + 4 * images + b])
        for b in range(own_images)
    ]
    for c in c1 + c1_own:
        c.start()
    for g in range(1, images):
        for c in qkv[g]:
            c.start()

    scale = HEAD_DIM ** (-0.5) * math.log2(math.e)
    block = math.gcd(length, 256)
    o_copies = []
    o_mine = []

    def attend(g):
        for c in qkv[g]:
            c.wait_recv()
        for a in range(3):
            mine[3 * g + a].wait()
        for h in range(heads):
            vx[h, :, 0:HEAD_DIM] = vb[g, :, h * HEAD_DIM : (h + 1) * HEAD_DIM]
            if g == 0:
                vx[h, :, HEAD_DIM : 2 * HEAD_DIM] = jnp.ones((length, HEAD_DIM), BF16)

        @pl.loop(0, length // block)
        def _(j):
            rows = pl.ds(pl.multiple_of(j * block, block), block)
            for h in range(heads):
                cols = slice(h * HEAD_DIM, (h + 1) * HEAD_DIM)
                scores = lax.dot_general(
                    qb[g, rows, cols], kb[g, :, cols], (((1,), (1,)), ((), ())),
                    preferred_element_type=F32,
                )
                peak = jnp.max(scores, axis=1, keepdims=True)
                weights = jnp.exp2((scores - peak) * scale).astype(BF16)
                mixed = jnp.dot(weights, vx[h], preferred_element_type=F32)
                ob[g, rows, cols] = (mixed[:, :HEAD_DIM] / mixed[:, HEAD_DIM:]).astype(BF16)

        for i, p in enumerate(seq_peers):
            c = rem(ob.at[g, aligned(p, own_tokens), :], att_ref.at[g, :, aligned(s, hw)],
                    o_s.at[g, i], o_r.at[g, i], z, p)
            c.start()
            o_copies.append(c)
        c = pltpu.make_async_copy(
            ob.at[g, aligned(s, own_tokens), :], att_ref.at[g, :, aligned(s, hw)],
            loc.at[5 + 3 * images + g])
        c.start()
        o_mine.append(c)

    attend(0)

    for c in wz:
        c.wait_recv()
    local[0].wait()

    def rows_to(first, last, origin, ss, rs, to):
        ref = wcf_ref.at[first:last, origin]
        return rem(ref, ref, ss, rs, z, to)

    relayed = n_seq == 8
    if relayed:
        side = s + 2 - 4 * lax.rem(s // 2, 2)
        across = s + 4 - 8 * (s // 4)
        chip_peers = [side, across]
        origins = [side, across, side + across - s]
    else:
        chip_peers = [lax.rem(s + 2 * j, n_seq) for j in range(1, n_seq // 2)]
        origins = [lax.rem(s + n_seq - 2 * j, n_seq) for j in range(1, n_seq // 2)]
    wp = [rows_to(0, n_ctl, s, wp_s.at[i], wp_r.at[i], p) for i, p in enumerate(chip_peers)]
    for c in wp:
        c.start()
    wf = [rows_to(0, n_ctl, s, wf_s.at[0], wf_r.at[0], sib)]
    wf[0].start()

    for c in c1:
        c.wait_recv()
    for c in c1_own:
        c.wait()
    pair = c1_ref.shape[0] // n_ctl
    c2 = [
        rem(c1_ref.at[pl.ds(p * pair, pair)], xr.at[z], c2_s.at[i], c2_r.at[i], p, s)
        for i, p in enumerate(ctl_peers)
    ]
    for c in c2:
        c.start()
    c2_own = pltpu.make_async_copy(
        c1_ref.at[pl.ds(z * pair, pair)], xr.at[z], loc.at[4 + 3 * images])
    c2_own.start()
    both(az_arrived, 1, "wait")
    local[1].wait()
    local[2].wait()
    if n_ctl > 2:
        both(az, 2, "start")

    for g in range(1, images):
        attend(g)

    wr = []
    half = n_ctl // 2
    for i, c in enumerate(wp):
        c.wait_recv()
        if relayed:
            first, last = ((0, half), (half, n_ctl))[i]
            c = rows_to(first, last, chip_peers[i], wr_s.at[i], wr_r.at[i], chip_peers[1 - i])
            c.start()
            wr.append(c)
    for i in range(len(wp)):
        c = rows_to(0, n_ctl, origins[i], wf_s.at[i + 1], wf_r.at[i + 1], sib)
        c.start()
        wf.append(c)
    both(az_arrived, 1, "pass")
    for step in range(2, n_ctl):
        both(az_arrived, step, "wait")
        if step + 1 < n_ctl:
            both(az, step + 1, "start")
        both(az_arrived, step, "pass")
    for c in wr:
        c.wait_recv()
    if relayed:
        c = rows_to(0, n_ctl, origins[2], wf_s.at[3], wf_r.at[3], sib)
        c.start()
        wf.append(c)

    for c in c2:
        c.wait_recv()
    c2_own.wait()
    for c in c1:
        c.wait_send()
    tile = wb.shape[4]
    tokens = nrm.shape[0] * nrm.shape[1]

    @pl.loop(0, width // tile)
    def _(j):
        cols = aligned(j, tile)
        x = xr[:, :, :, cols].reshape(tokens, tile)
        y = jnp.dot(order_ref[...], x, preferred_element_type=F32)
        nrm[:, :, cols] = y.astype(BF16).reshape(nrm.shape[0], nrm.shape[1], tile)

    for c in wf:
        c.wait_recv()

    def w_copy(j, slot):
        return pltpu.make_async_copy(
            wcf_ref.at[:, :, :, aligned(j, tile)], wb.at[slot], ws.at[slot])

    w_copy(0, 0).start()

    @pl.loop(0, width // tile)
    def _(j):
        slot = lax.rem(j, 2)

        @pl.when(j + 1 < width // tile)
        def _():
            w_copy(j + 1, 1 - slot).start()

        w_copy(j, slot).wait()
        y = jnp.dot(
            nrm[...].reshape(tokens, width), wb[slot].reshape(width, tile),
            preferred_element_type=F32,
        )
        xr[:, :, :, aligned(j, tile)] = y.astype(BF16).reshape(xr.shape[:3] + (tile,))

    done = pltpu.make_async_copy(xr, res_ref, loc.at[3])
    done.start()

    for c in o_copies:
        c.wait_recv()
    for c in o_mine:
        c.wait()
    for step in range(1, n_ctl):
        both(az_arrived, step, "passed")
        both(az_arrived, step, "sent")
        both(az, step, "sent")
    for c in wz + c2 + wp + wr + wf + o_copies:
        c.wait_send()
    for g in range(images):
        for c in qkv[g]:
            c.wait_send()
    done.wait()


def exchange(q, k, v, hidden, wc, wa, seg, dep, table, depth_base, gain_rows, order, n_ctl, n_seq):
    images, own_tokens, inner = q.shape
    length = own_tokens * n_seq
    hw = inner // n_seq
    own_images, grid_rows, grid_cols, width = hidden.shape
    part = grid_rows // n_seq
    ct = part * grid_cols
    total = own_images * n_seq
    pair = total // n_ctl
    tile = math.gcd(width, 256)
    wc_rows = wc.shape[0] // n_seq
    dma = lambda *shape: pltpu.SemaphoreType.DMA(shape)
    anywhere = pl.BlockSpec(memory_space=pl.ANY)
    held = pl.BlockSpec(memory_space=pltpu.VMEM)
    flops = 4 * images * length * length * hw
    return pl.pallas_call(
        functools.partial(exchange_kernel, n_ctl, n_seq, depth_base),
        out_shape=[
            jax.ShapeDtypeStruct(q.shape, BF16),
            jax.ShapeDtypeStruct((n_ctl, pair, ct, width), BF16),
            jax.ShapeDtypeStruct((total, ct, width), BF16),
            jax.ShapeDtypeStruct((n_ctl, n_seq, wc_rows, width), BF16),
            jax.ShapeDtypeStruct((n_ctl, 2, wa.shape[0] // 2, wa.shape[1]), BF16),
        ],
        in_specs=[anywhere] * 6 + [held] * 5,
        out_specs=[anywhere] * 5,
        scratch_shapes=[
            pltpu.VMEM((images, length, hw), BF16),
            pltpu.VMEM((images, length, hw), BF16),
            pltpu.VMEM((images, length, hw), BF16),
            pltpu.VMEM((hw // HEAD_DIM, length, 2 * HEAD_DIM), BF16),
            pltpu.VMEM((images, length, hw), BF16),
            pltpu.VMEM((2, part, grid_cols, width), BF16),
            pltpu.VMEM((ct, width), F32),
            pltpu.VMEM((total, ct, width), BF16),
            pltpu.VMEM((n_ctl, pair, ct, width), BF16),
            pltpu.VMEM((2, n_ctl, n_seq, wc_rows, tile), BF16),
            dma(images, 3, n_seq - 1), dma(images, 3, n_seq - 1),
            dma(images, n_seq - 1), dma(images, n_seq - 1),
            dma(own_images, n_seq - 1), dma(own_images, n_seq - 1),
            dma(n_ctl - 1), dma(n_ctl - 1),
            dma(n_ctl - 1), dma(n_ctl - 1),
            dma(n_seq // 2), dma(n_seq // 2),
            dma(2), dma(2),
            dma(n_seq // 2), dma(n_seq // 2),
            dma(2, n_ctl - 1), dma(2, n_ctl - 1),
            dma(2, n_ctl - 1), dma(2, n_ctl - 1),
            dma(5 + 4 * images + own_images),
            dma(2),
            dma(2),
        ],
        compiler_params=pltpu.CompilerParams(
            collective_id=0, has_side_effects=True, vmem_limit_bytes=56 * 2**20
        ),
        cost_estimate=pl.CostEstimate(
            flops=flops, bytes_accessed=64 * 2**20, transcendentals=images * length * length * 2
        ),
    )(
        q, k, v, hidden, wc, wa,
        seg.reshape(total, ct, 1), dep.reshape(total, ct, 1), table, gain_rows[:, None, :], order,
    )


def per_device(
    n_ctl, n_seq,
    control_hidden_state,
    patch_segment_labels,
    patch_depth_levels,
    timestep,
    segment_label_embedding,
    depth_level_embedding,
    timestep_weight,
    control_norm_gain,
    control_output_weight,
    transformer_hidden_state,
    query,
    key,
    value,
    attention_output_weight,
):
    gain = time_embed(timestep, timestep_weight)
    own_images, _, ctl_cols, width = control_hidden_state.shape
    ctl_gain = lax.dynamic_slice_in_dim(gain, lax.axis_index("seq") * own_images, own_images, 0)
    images, rows, cols, inner = query.shape
    tokens = rows * cols
    flat = lambda a: a.reshape(images, tokens, inner)
    out_index = jnp.arange(images * tokens, dtype=jnp.int32)
    image, place = out_index // tokens, out_index % tokens
    row, col = place // cols, place % cols
    source = (
        ((col // ctl_cols) * images + image) * (rows * ctl_cols) + row * ctl_cols + col % ctl_cols
    )
    order = (source[:, None] == out_index[None, :]).astype(BF16)
    depth_base = -(-segment_label_embedding.shape[0] // 256) * 256
    table = jnp.concatenate(
        [
            jnp.pad(
                segment_label_embedding,
                ((0, depth_base - segment_label_embedding.shape[0]), (0, 0)),
            ),
            depth_level_embedding,
        ],
        axis=0,
    )
    attended, residual, _, _, wa_full = exchange(
        flat(query), flat(key), flat(value), control_hidden_state,
        control_output_weight, attention_output_weight,
        patch_segment_labels, patch_depth_levels, table, depth_base,
        control_norm_gain * (1.0 + ctl_gain), order, n_ctl, n_seq,
    )
    projected = jnp.dot(
        attended.reshape(images * tokens, inner),
        wa_full.reshape(inner, width),
        preferred_element_type=F32,
    )
    t_gain = lax.dynamic_slice_in_dim(gain, lax.axis_index("ctl") * images, images, 0)
    shape = (images, tokens, width)
    final = (
        transformer_hidden_state.reshape(shape).astype(F32)
        + t_gain[:, None, :] * projected.reshape(shape)
        + residual.reshape(shape).astype(F32)
    )
    return final.astype(BF16).reshape(transformer_hidden_state.shape)


def solution(mesh):
    return jax.shard_map(
        functools.partial(per_device, mesh.shape["ctl"], mesh.shape["seq"]),
        mesh=mesh,
        in_specs=(
            P("seq", None, "ctl", None),
            P("seq", None, "ctl"),
            P("seq", None, "ctl"),
            P(),
            P(),
            P(),
            P(),
            P(),
            P("ctl", None),
            P("ctl", "seq", None, None),
            P("ctl", "seq", None, None),
            P("ctl", "seq", None, None),
            P("ctl", "seq", None, None),
            P("ctl", None),
        ),
        out_specs=P("ctl", "seq", None, None),
        check_vma=False,
    )
```

time: 366 us -> 334 us (0.913)
  matrix products: 47.3 us -> 17 us
  Pallas kernels: 304 us -> 300 us
    dot_general x1 -> x0, matrix products: 28.4 us -> none  [per_device(): jnp.dot(normed_rows, wc_full.reshape(-1, width), preferred_element_type=F32)]
    pallas_call x2 -> x1, Pallas kernels: 304 us -> 300 us  [exchange(): pl.pallas_call(functools.partial(exchange_kernel, n_ctl, n_seq, depth_bas...]
    unnamed x9 -> x15, local copies, waits for them, and re-layouts: 7.72 us -> 6.96 us
where the time goes in v2:
time: 334 us
  Pallas kernels  300 us (90%)
  matrix products  17 us (5%)
  local copies, waits for them, and re-layouts  8.8 us (3%)
  other arithmetic  7.38 us (2%)
    pallas_call x1, Pallas kernels, exchange(): pl.pallas_call(functools.partial(exchange_kernel, n_ctl, n_seq, depth_bas...  300 us
    dot_general x1, matrix products, per_device(): jnp.dot(attended.reshape(images * tokens, inner), wa_full.reshape(inner,...  16.7 us
    unnamed x15, local copies, waits for them, and re-layouts  6.96 us

profile of v2, /device:TPU:0, one launch (start us, length us, event | category | flops | bytes accessed | tf_op | source)
XLA Modules:
  0.0 333.6 jit_solution(16110485422078845818)
XLA Ops:
  0.0 0.0 copy-start
  0.0 0.0 copy-start.3
  0.0 0.8 convert_element_type.26
  0.8 0.1 fusion.14
  1.0 0.8 copy.18
  1.8 0.8 copy.19
  2.5 0.0 copy-done
  2.5 0.3 divide_multiply_fusion
  2.9 1.3 multiply_bitcast_fusion.gain_ref
  4.2 0.9 reshape.96.dep_ref
  5.1 0.9 reshape.95.seg_ref
  6.0 0.0 copy-start.2
  6.0 1.3 fusion.3.order_ref
  7.3 0.0 copy-done.3
  7.3 3.8 %fusion.2.table_ref = bf16[512,3072]{1,0:T(8,128)(2,1)} fusion(bf16[150,3072]{1,0:T(8,128)(2,1)} %param.18, bf16[256,3072]{1,0:T(8,128)(2,1)S(1)} %copy-done.3), kind=kLoop, calls=%fused_computation.5 | loop fusion | flops 9437184 | bytes 5640192 | tf_op jit(solution)/shard_map/concatenate | solution.py:444
  11.1 0.0 copy-done.2
  11.1 0.0 slice-start
  11.1 5.4 %copy.20.x_ref = bf16[1,64,12,3072]{3,2,1,0:T(8,128)(2,1)} copy(bf16[1,64,12,3072]{3,1,2,0:T(8,128)(2,1)S(1)} %copy-done.2) | data formatting | bytes 9437184 | tf_op args[0]
  16.5 0.0 slice-start.1
  16.5 300.4 %shard_map.136 = (bf16[2,384,2048]{2,1,0:T(8,128)(2,1)}, bf16[4,2,96,3072]{3,2,1,0:T(8,128)(2,1)}, bf16[8,96,3072]{2,1,0:T(8,128)(2,1)}, bf16[4,8,96,3072]{3,2,1,0:T(8,128)(2,1)}, bf16[4,2,256,3072]{3,2,1,0:T(8,128)(2,1)}) custom-call(bf16[2,384,2048]{2,1,0:T(8,128)(2,1)} %bitcast.21, bf16[2,384,2048]{2,1,0:T(8,128)(2,1)} %bitcast.22, ...), custom_call_target="tpu_custom_call" | custom-call | flops 19327352832 | bytes 67108864 | tf_op jit(solution)/shard_map/pallas_call | solution.py:365
  316.9 0.0 slice-done
  316.9 0.0 slice-done.1
  316.9 0.0 copy-start.1
  317.0 16.7 %fusion = bf16[2,384,3072]{2,1,0:T(8,128)(2,1)} fusion(bf16[2,384,3072]{2,1,0:T(8,128)(2,1)} %bitcast.25, bf16[2,384,3072]{2,1,0:T(8,128)(2,1)S(1)} %bitcast.20, bf16[2,384,2048]{2,1,0:T(8,128)(2,1)} %get-tuple-element.8, bf16[2048,3072,1]{1,0,2:T(8,128)(2,1)} %bitcast.24, f32[2,3072]{1,0:T(2,128)S(1)} %constant_dynamic-slice_fusion), kind=kOutput, calls=%fused_computation.1 | convolution fusion | flops 9677832192 | bytes 29908992 | tf_op jit(solution)/shard_map/dot_general | solution.py:460
  333.6 0.0 copy-done.1
  (4 shorter events, 0.1 us)
Async XLA Ops:
  0.0 2.5 copy-start
  0.0 7.3 %copy-start.3 = (bf16[256,3072]{1,0:T(8,128)(2,1)S(1)}, bf16[256,3072]{1,0:T(8,128)(2,1)}, u32[]{:S(2)}) copy-start(bf16[256,3072]{1,0:T(8,128)(2,1)} %param.19) | copy-start | bytes 4718596
  6.0 5.1 %copy-start.2 = (bf16[1,64,12,3072]{3,1,2,0:T(8,128)(2,1)S(1)}, bf16[1,64,12,3072]{3,1,2,0:T(8,128)(2,1)}, u32[]{:S(2)}) copy-start(bf16[1,64,12,3072]{3,1,2,0:T(8,128)(2,1)} %param.14) | copy-start | bytes 14155780
  11.1 305.8 %slice-start = ((s8[4718592]{0:T(1024)(128)(4,1)}), s8[4194304]{0:T(1024)(128)(4,1)S(1)}, s32[]{:S(2)}) async-start(s8[4718592]{0:T(1024)(128)(4,1)} %bitcast.18), calls=%async_computation | async-start | bytes 8388608
  16.5 300.4 %slice-start.1 = ((s8[4718592]{0:T(1024)(128)(4,1)}), s8[524288]{0:T(1024)(128)(4,1)S(1)}, s32[]{:S(2)}) async-start(s8[4718592]{0:T(1024)(128)(4,1)} %bitcast.18), calls=%async_computation.1 | async-start | bytes 1048576
  316.9 16.7 %copy-start.1 = (bf16[256,3072]{1,0:T(8,128)(2,1)S(1)}, bf16[256,3072]{1,0:T(8,128)(2,1)}, u32[]{:S(2)}) copy-start(bf16[256,3072]{1,0:T(8,128)(2,1)} %param.20) | copy-start | bytes 4718596

commit v3 on v2

--- a/solution.py
+++ b/solution.py
@@ -122,18 +122,20 @@
         for a, (src, dst) in enumerate(((q_ref, qb), (k_ref, kb), (v_ref, vb)))
     ]
 
-    for c in wz + qkv[0]:
+    first_q = n_seq - 1
+    for c in wz + qkv[0][:first_q]:
         c.start()
     both(az, 1, "start")
 
-    own_images, grid_rows, grid_cols = x_ref.shape[0], x_ref.shape[1], x_ref.shape[2]
+    own_images, grid_cols, grid_rows = x_ref.shape[0], x_ref.shape[1], x_ref.shape[2]
     part = grid_rows // n_seq
     ct = part * grid_cols
-    groups = own_images * n_seq
+    halves = n_seq // 2
+    groups = own_images * halves
 
     def x_copy(t, slot):
         return pltpu.make_async_copy(
-            x_ref.at[t // n_seq, pl.ds(lax.rem(t, n_seq) * part, part)], xb.at[slot], xs.at[slot])
+            x_ref.at[t // halves, :, aligned(lax.rem(t, halves), 2 * part), :], xb.at[slot], xs.at[slot])
 
     x_copy(0, 0).start()
     for c in local + mine:
@@ -148,14 +150,18 @@
             x_copy(t + 1, 1 - slot).start()
 
         x_copy(t, slot).wait()
-        for r in range(part):
-            rows_f[r * grid_cols : (r + 1) * grid_cols, :] = xb[slot, r].astype(F32)
+        for c in range(grid_cols):
+            both_rows = xb[slot, c].astype(F32)
+            for u in range(2):
+                rows_f[u, c * part : (c + 1) * part, :] = both_rows[u * part : (u + 1) * part]
         iota = lax.broadcasted_iota(jnp.int32, (ct, table_ref.shape[0]), 1)
-        hit = jnp.logical_or(iota == seg_ref[t], iota == dep_ref[t] + depth_base)
-        onehot = jnp.where(hit, 1.0, 0.0).astype(BF16)
-        mixed = rows_f[...] + jnp.dot(onehot, table_ref[...], preferred_element_type=F32)
-        norm = lax.rsqrt(jnp.mean(mixed * mixed, axis=-1, keepdims=True) + 1e-06)
-        nrm[t] = (mixed * norm * gain_ref[t // n_seq]).astype(BF16)
+        for u in range(2):
+            g = 2 * t + u
+            hit = jnp.logical_or(iota == seg_ref[g], iota == dep_ref[g] + depth_base)
+            onehot = jnp.where(hit, 1.0, 0.0).astype(BF16)
+            mixed = rows_f[u] + jnp.dot(onehot, table_ref[...], preferred_element_type=F32)
+            norm = lax.rsqrt(jnp.mean(mixed * mixed, axis=-1, keepdims=True) + 1e-06)
+            nrm[g] = (mixed * norm * gain_ref[t // halves]).astype(BF16)
 
     c1 = [
         [
@@ -169,11 +175,55 @@
         pltpu.make_async_copy(nrm.at[b * n_seq + s], c1_ref.at[s * own_images + b], loc.at[5 + 4 * images + b])
         for b in range(own_images)
     ]
-    for c in c1 + c1_own:
-        c.start()
+    for c in c1 + c1_own + qkv[0][first_q:]:
+        c.start()
+
+    for c in c1:
+        c.wait_recv()
+    for c in c1_own:
+        c.wait()
+    pair = c1_ref.shape[0] // n_ctl
+    c2 = [
+        rem(c1_ref.at[pl.ds(p * pair, pair)], xr.at[z], c2_s.at[i], c2_r.at[i], p, s)
+        for i, p in enumerate(ctl_peers)
+    ]
+    for c in c2:
+        c.start()
+    c2_own = pltpu.make_async_copy(
+        c1_ref.at[pl.ds(z * pair, pair)], xr.at[z], loc.at[4 + 3 * images])
+    c2_own.start()
     for g in range(1, images):
         for c in qkv[g]:
             c.start()
+    both(az_arrived, 1, "wait")
+    local[1].wait()
+    local[2].wait()
+    if n_ctl > 2:
+        both(az, 2, "start")
+
+
+    for c in wz:
+        c.wait_recv()
+    local[0].wait()
+
+    def rows_to(first, last, origin, ss, rs, to):
+        ref = wcf_ref.at[first:last, origin]
+        return rem(ref, ref, ss, rs, z, to)
+
+    relayed = n_seq == 8
+    if relayed:
+        side = s + 2 - 4 * lax.rem(s // 2, 2)
+        across = s + 4 - 8 * (s // 4)
+        chip_peers = [side, across]
+        origins = [side, across, side + across - s]
+    else:
+        chip_peers = [lax.rem(s + 2 * j, n_seq) for j in range(1, n_seq // 2)]
+        origins = [lax.rem(s + n_seq - 2 * j, n_seq) for j in range(1, n_seq // 2)]
+    wp = [rows_to(0, n_ctl, s, wp_s.at[i], wp_r.at[i], p) for i, p in enumerate(chip_peers)]
+    for c in wp:
+        c.start()
+    wf = [rows_to(0, n_ctl, s, wf_s.at[0], wf_r.at[0], sib)]
+    wf[0].start()
 
     scale = HEAD_DIM ** (-0.5) * math.log2(math.e)
     block = math.gcd(length, 256)
@@ -215,52 +265,7 @@
         c.start()
         o_mine.append(c)
 
-    attend(0)
-
-    for c in wz:
-        c.wait_recv()
-    local[0].wait()
-
-    def rows_to(first, last, origin, ss, rs, to):
-        ref = wcf_ref.at[first:last, origin]
-        return rem(ref, ref, ss, rs, z, to)
-
-    relayed = n_seq == 8
-    if relayed:
-        side = s + 2 - 4 * lax.rem(s // 2, 2)
-        across = s + 4 - 8 * (s // 4)
-        chip_peers = [side, across]
-        origins = [side, across, side + across - s]
-    else:
-        chip_peers = [lax.rem(s + 2 * j, n_seq) for j in range(1, n_seq // 2)]
-        origins = [lax.rem(s + n_seq - 2 * j, n_seq) for j in range(1, n_seq // 2)]
-    wp = [rows_to(0, n_ctl, s, wp_s.at[i], wp_r.at[i], p) for i, p in enumerate(chip_peers)]
-    for c in wp:
-        c.start()
-    wf = [rows_to(0, n_ctl, s, wf_s.at[0], wf_r.at[0], sib)]
-    wf[0].start()
-
-    for c in c1:
-        c.wait_recv()
-    for c in c1_own:
-        c.wait()
-    pair = c1_ref.shape[0] // n_ctl
-    c2 = [
-        rem(c1_ref.at[pl.ds(p * pair, pair)], xr.at[z], c2_s.at[i], c2_r.at[i], p, s)
-        for i, p in enumerate(ctl_peers)
-    ]
-    for c in c2:
-        c.start()
-    c2_own = pltpu.make_async_copy(
-        c1_ref.at[pl.ds(z * pair, pair)], xr.at[z], loc.at[4 + 3 * images])
-    c2_own.start()
-    both(az_arrived, 1, "wait")
-    local[1].wait()
-    local[2].wait()
-    if n_ctl > 2:
-        both(az, 2, "start")
-
-    for g in range(1, images):
+    for g in range(images):
         attend(g)
 
     wr = []
@@ -277,10 +282,9 @@
         c.start()
         wf.append(c)
     both(az_arrived, 1, "pass")
-    for step in range(2, n_ctl):
+    for step in range(2, n_ctl - 1):
         both(az_arrived, step, "wait")
-        if step + 1 < n_ctl:
-            both(az, step + 1, "start")
+        both(az, step + 1, "start")
         both(az_arrived, step, "pass")
     for c in wr:
         c.wait_recv()
@@ -330,6 +334,10 @@
 
     done = pltpu.make_async_copy(xr, res_ref, loc.at[3])
     done.start()
+
+    if n_ctl > 2:
+        both(az_arrived, n_ctl - 1, "wait")
+        both(az_arrived, n_ctl - 1, "pass")
 
     for c in o_copies:
         c.wait_recv()
@@ -362,6 +370,11 @@
     anywhere = pl.BlockSpec(memory_space=pl.ANY)
     held = pl.BlockSpec(memory_space=pltpu.VMEM)
     flops = 4 * images * length * length * hw
+
+    def by_column(labels):
+        labels = labels.reshape(own_images, n_seq, part, grid_cols)
+        return jnp.transpose(labels, (0, 1, 3, 2)).reshape(total, ct, 1)
+
     return pl.pallas_call(
         functools.partial(exchange_kernel, n_ctl, n_seq, depth_base),
         out_shape=[
@@ -379,8 +392,8 @@
             pltpu.VMEM((images, length, hw), BF16),
             pltpu.VMEM((hw // HEAD_DIM, length, 2 * HEAD_DIM), BF16),
             pltpu.VMEM((images, length, hw), BF16),
-            pltpu.VMEM((2, part, grid_cols, width), BF16),
-            pltpu.VMEM((ct, width), F32),
+            pltpu.VMEM((2, grid_cols, 2 * part, width), BF16),
+            pltpu.VMEM((2, ct, width), F32),
             pltpu.VMEM((total, ct, width), BF16),
             pltpu.VMEM((n_ctl, pair, ct, width), BF16),
             pltpu.VMEM((2, n_ctl, n_seq, wc_rows, tile), BF16),
@@ -405,8 +418,7 @@
             flops=flops, bytes_accessed=64 * 2**20, transcendentals=images * length * length * 2
         ),
     )(
-        q, k, v, hidden, wc, wa,
-        seg.reshape(total, ct, 1), dep.reshape(total, ct, 1), table, gain_rows[:, None, :], order,
+        q, k, v, jnp.transpose(hidden, (0, 2, 1, 3)), wc, wa, by_column(seg), by_column(dep), table, gain_rows[:, None, :], order,
     )
 
 
@@ -437,7 +449,7 @@
     image, place = out_index // tokens, out_index % tokens
     row, col = place // cols, place % cols
     source = (
-        ((col // ctl_cols) * images + image) * (rows * ctl_cols) + row * ctl_cols + col % ctl_cols
+        ((col // ctl_cols) * images + image) * (rows * ctl_cols) + (col % ctl_cols) * rows + row
     )
     order = (source[:, None] == out_index[None, :]).astype(BF16)
     depth_base = -(-segment_label_embedding.shape[0] // 256) * 256

time: 334 us -> 329 us (0.985)
  local copies, waits for them, and re-layouts: 8.8 us -> 2.01 us
    unnamed x15 -> x10, local copies, waits for them, and re-layouts: 6.96 us -> 0.02 us
where the time goes in v3:
time: 329 us; the launch traced here: 328 us
  Pallas kernels  301 us (91%)
  matrix products  16.9 us (5%)
  other arithmetic  8.4 us (3%)
    pallas_call x1, Pallas kernels, exchange(): pl.pallas_call(functools.partial(exchange_kernel, n_ctl, n_seq, depth_bas...  301 us
    dot_general x1, matrix products, per_device(): jnp.dot(attended.reshape(images * tokens, inner), wa_full.reshape(inner,...  16.6 us

profile of v3, /device:TPU:0, one launch (start us, length us, event | category | flops | bytes accessed | tf_op | source)
XLA Modules:
  0.0 328.1 jit_solution(11893521080925184587)
XLA Ops:
  0.0 0.0 copy-start
  0.0 0.0 copy-start.2
  0.0 0.8 convert_element_type.26
  0.8 0.1 fusion.14
  1.0 0.7 reduce
  1.7 0.7 reduce.1
  2.4 0.1 reshape.96
  2.5 0.1 reshape.94
  2.6 0.0 copy-done
  2.6 0.3 divide_multiply_fusion
  3.0 1.3 multiply_bitcast_fusion.gain_ref
  4.3 0.9 reshape.103.seg_ref
  5.2 0.9 reshape.104.dep_ref
  6.1 1.3 fusion.3.order_ref
  7.4 0.0 copy-done.2
  7.4 0.0 slice-start
  7.4 3.4 %fusion.2.table_ref = bf16[512,3072]{1,0:T(8,128)(2,1)} fusion(bf16[150,3072]{1,0:T(8,128)(2,1)} %param.18, bf16[256,3072]{1,0:T(8,128)(2,1)S(1)} %copy-done.2), kind=kLoop, calls=%fused_computation.5 | loop fusion | flops 9437184 | bytes 5640192 | tf_op jit(solution)/shard_map/concatenate | solution.py:456
  10.8 0.0 slice-start.1
  10.8 300.7 %shard_map.136 = (bf16[2,384,2048]{2,1,0:T(8,128)(2,1)}, bf16[4,2,96,3072]{3,2,1,0:T(8,128)(2,1)}, bf16[8,96,3072]{2,1,0:T(8,128)(2,1)}, bf16[4,8,96,3072]{3,2,1,0:T(8,128)(2,1)}, bf16[4,2,256,3072]{3,2,1,0:T(8,128)(2,1)}) custom-call(bf16[2,384,2048]{2,1,0:T(8,128)(2,1)} %bitcast.31, bf16[2,384,2048]{2,1,0:T(8,128)(2,1)} %bitcast.32, ...), custom_call_target="tpu_custom_call" | custom-call | flops 19327352832 | bytes 67108864 | tf_op jit(solution)/shard_map/pallas_call | solution.py:378
  311.5 0.0 slice-done
  311.5 0.0 slice-done.1
  311.5 0.0 copy-start.1
  311.5 16.6 %fusion = bf16[2,384,3072]{2,1,0:T(8,128)(2,1)} fusion(bf16[2,384,3072]{2,1,0:T(8,128)(2,1)} %bitcast.35, bf16[2,384,3072]{2,1,0:T(8,128)(2,1)S(1)} %bitcast.30, bf16[2,384,2048]{2,1,0:T(8,128)(2,1)} %get-tuple-element.8, bf16[2048,3072,1]{1,0,2:T(8,128)(2,1)} %bitcast.34, f32[2,3072]{1,0:T(2,128)S(1)} %constant_dynamic-slice_fusion), kind=kOutput, calls=%fused_computation.1 | convolution fusion | flops 9677832192 | bytes 29908992 | tf_op jit(solution)/shard_map/dot_general | solution.py:472
  328.1 0.0 copy-done.1
  (6 shorter events, 0.1 us)
Async XLA Ops:
  0.0 2.6 copy-start
  0.0 7.4 %copy-start.2 = (bf16[256,3072]{1,0:T(8,128)(2,1)S(1)}, bf16[256,3072]{1,0:T(8,128)(2,1)}, u32[]{:S(2)}) copy-start(bf16[256,3072]{1,0:T(8,128)(2,1)} %param.19) | copy-start | bytes 4718596
  7.4 304.1 %slice-start = ((s8[4718592]{0:T(1024)(128)(4,1)}), s8[4194304]{0:T(1024)(128)(4,1)S(1)}, s32[]{:S(2)}) async-start(s8[4718592]{0:T(1024)(128)(4,1)} %bitcast.28), calls=%async_computation | async-start | bytes 8388608
  10.8 300.7 %slice-start.1 = ((s8[4718592]{0:T(1024)(128)(4,1)}), s8[524288]{0:T(1024)(128)(4,1)S(1)}, s32[]{:S(2)}) async-start(s8[4718592]{0:T(1024)(128)(4,1)} %bitcast.28), calls=%async_computation.1 | async-start | bytes 1048576
  311.5 16.6 %copy-start.1 = (bf16[256,3072]{1,0:T(8,128)(2,1)S(1)}, bf16[256,3072]{1,0:T(8,128)(2,1)}, u32[]{:S(2)}) copy-start(bf16[256,3072]{1,0:T(8,128)(2,1)} %param.20) | copy-start | bytes 4718596
